TPU v7x, 128 devices: a whole 4x4x4 slice. The times are simulated.
128 devices in a mesh: dp: 8 (over x, core), ep: 16 (over z, y).
Axes of the slice: x: 4, y: 4, z: 4, core: 2. Of those that a mesh axis runs over, the one named last changes fastest.
Arguments:
- hidden: bfloat16 [256, 7168], P(('dp', 'ep')), may hold values from -20 to 20
- q_latent: bfloat16 [256, 64, 512], P(('dp', 'ep')), may hold values from -48 to 48
- q_rope: bfloat16 [256, 64, 64], P(('dp', 'ep')), may hold values from -48 to 48
- latent_pages: bfloat16 [3072, 64, 512], P(('dp', 'ep')), may hold values from -8 to 8
- rope_pages: bfloat16 [3072, 32, 128], P(('dp', 'ep')), may hold values from -8 to 8
- block_table: int32 [256, 12], P(('dp', 'ep')), may hold values from 0 to 23, as said below
- cache_len: int32 [256], P(('dp', 'ep')), may hold values from 2 to 768, as said below
- move_req: int32 [128], P(('dp', 'ep')), may hold values from 0 to 1, as said below
- move_to: int32 [128], P(('dp', 'ep')), may hold values from 0 to 7, as said below
- routing: int32 [256, 8], P(('dp', 'ep')), may hold values from 0 to 15, all different within a row; in each aligned block of 2 rows (0 to 1, 2 to 3, ...) at most 2 rows name the same one
- gate_weight: float32 [256, 8], P(('dp', 'ep')), may hold values from 0.1 to 1
- norm_gain: float32 [7168], replicated, may hold values from 0.1 to 1.9
- w_uv: bfloat16 [64, 512, 128], P('ep'), may hold values from -0.25 to 0.25
- w_out: bfloat16 [8192, 7168], P('ep'), may hold values from -0.5 to 0.5
- w_gate: bfloat16 [16, 7168, 2048], P('ep', None, 'dp'), may hold values from -0.0625 to 0.0625
- w_up: bfloat16 [16, 7168, 2048], P('ep', None, 'dp'), may hold values from -0.0625 to 0.0625
- w_down: bfloat16 [16, 2048, 7168], P('ep', 'dp'), may hold values from -0.125 to 0.125
Outputs:
- mixed: bfloat16 [256, 7168], P(('dp', 'ep'))
Inputs may be any that keep to these rules, and one draw needn't show every extreme that they name: `block_table`: each row names pages of its home device's own block of 24 pages by their index within that block; no page is named twice. `cache_len`: every handed-off request has exactly 768 cache positions. `move_req`: every device hands off exactly one request. `move_to`: among the devices of one ep index these dp indices form a permutation: each device hands off one request and receives one; a device may keep its own. `routing`: rows in the new layout. Each row names 8 different experts; among the rows of one device no expert is named more than 2 times, and some device reaches it.
All inputs are finite; a program needn't handle non-finite values.
Results may differ from a plain program's by a relative error of at most 0.023.
Values may be sent and summed in bfloat16 or wider, within the bound.
A program may use at most 128 MiB of HBM per device.

v0:
```python
import jax
import jax.numpy as jnp
from jax import lax
from jax.sharding import PartitionSpec as P


def pick_row(stacked, which_one):
    return lax.dynamic_index_in_dim(stacked, which_one, 0, keepdims=False)


def place_lane(single, lane_mask):
    shaped = lane_mask.reshape((lane_mask.shape[0],) + (1,) * single.ndim)
    return jnp.where(shaped, single[None], jnp.zeros_like(single)[None])


def merge_lanes(arrived):
    return jnp.sum(arrived.astype(jnp.float32), axis=0).astype(arrived.dtype)


def swap_slot(stacked, slot_mask, single):
    shaped = slot_mask.reshape((slot_mask.shape[0],) + (1,) * single.ndim)
    return jnp.where(shaped, single[None], stacked)


def on_device(
    hidden,
    q_latent,
    q_rope,
    latent_pages,
    rope_pages,
    block_table,
    cache_len,
    move_req,
    move_to,
    routing,
    gate_weight,
    norm_gain,
    w_uv,
    w_out,
    w_gate,
    w_up,
    w_down,
):
    requests = hidden.shape[0]
    model_width = hidden.shape[1]
    page_size = latent_pages.shape[1]
    latent_width = latent_pages.shape[2]
    rope_width = q_rope.shape[2]
    value_width = w_uv.shape[2]
    positions = block_table.shape[1] * page_size
    dp_count = lax.axis_size("dp")
    ep_count = lax.axis_size("ep")
    scale = (value_width + rope_width) ** (-0.5)
    latent_keys = latent_pages[block_table].reshape(requests, positions, latent_width)
    rope_keys = rope_pages.reshape(-1, page_size, rope_width)[block_table].reshape(
        requests, positions, rope_width
    )
    live = jnp.arange(positions)[None, :] < cache_len[:, None]
    leaving = move_req[0]
    target = move_to[0]
    slot_mask = jnp.arange(requests) == leaving
    lane_mask = jnp.arange(dp_count) == target
    scores = jnp.einsum("rhl,rtl->rht", q_latent, latent_keys, preferred_element_type=jnp.float32)
    scores = (
        scores + jnp.einsum("rhl,rtl->rht", q_rope, rope_keys, preferred_element_type=jnp.float32)
    ) * scale
    scores = jnp.where(live[:, None, :], scores, -jnp.inf)
    largest = jnp.max(scores, axis=2, keepdims=True)
    weights = jnp.exp(scores - largest)
    totals = jnp.sum(weights, axis=2, keepdims=True)
    latent_out = (
        jnp.einsum(
            "rht,rtl->rhl",
            weights.astype(jnp.bfloat16),
            latent_keys,
            preferred_element_type=jnp.float32,
        )
        / totals
    ).astype(jnp.bfloat16)
    by_heads = lax.all_to_all(latent_out, "ep", split_axis=1, concat_axis=0, tiled=True)
    values = jnp.einsum("ghl,hlv->ghv", by_heads, w_uv, preferred_element_type=jnp.float32).astype(
        jnp.bfloat16
    )
    values = values.reshape(values.shape[0], -1)
    attention = lax.psum_scatter(
        jnp.dot(values, w_out, preferred_element_type=jnp.float32).astype(jnp.bfloat16),
        "ep",
        scatter_dimension=0,
        tiled=True,
    ).astype(jnp.float32)
    attended = (hidden.astype(jnp.float32) + attention).astype(jnp.bfloat16)
    row_parcel = place_lane(pick_row(attended, leaving), lane_mask)
    arrived_rows = lax.all_to_all(row_parcel, "dp", split_axis=0, concat_axis=0, tiled=True)
    attended = swap_slot(attended, slot_mask, merge_lanes(arrived_rows))
    widened = attended.astype(jnp.float32)
    mean_square = jnp.mean(widened * widened, axis=1, keepdims=True)
    normed = (widened * lax.rsqrt(mean_square + 1e-06) * norm_gain).astype(jnp.bfloat16)
    top_count = routing.shape[1]
    capacity = min(requests, (requests * top_count + ep_count - 1) // ep_count + 1)
    onehot = (routing[:, :, None] == jnp.arange(ep_count, dtype=jnp.int32)[None, None, :]).astype(
        jnp.int32
    )
    named = jnp.sum(onehot, axis=1)
    slot_rank = jnp.cumsum(named, axis=0) - named
    position = (
        (slot_rank[:, :, None] == jnp.arange(capacity)[None, None, :]) & (named[:, :, None] > 0)
    ).astype(jnp.float32)
    gate_of = jnp.einsum(
        "rk,rke->re", gate_weight, onehot.astype(jnp.float32), precision=lax.Precision.HIGHEST
    )
    sending = jnp.einsum(
        "rec,rd->ecd", position.astype(jnp.bfloat16), normed, preferred_element_type=jnp.float32
    ).astype(jnp.bfloat16)
    combining = gate_of[:, :, None] * position
    spread = jnp.broadcast_to(sending[None], (dp_count,) + sending.shape).reshape(
        dp_count * ep_count, capacity, model_width
    )
    arrived_rows = lax.all_to_all(spread, ("dp", "ep"), split_axis=0, concat_axis=0, tiled=True)
    flat_rows = arrived_rows.reshape(-1, model_width)
    gated = jnp.dot(flat_rows, w_gate[0], preferred_element_type=jnp.float32)
    upward = jnp.dot(flat_rows, w_up[0], preferred_element_type=jnp.float32)
    inner = (jax.nn.silu(gated) * upward).astype(jnp.bfloat16)
    partial_out = jnp.dot(inner, w_down[0], preferred_element_type=jnp.float32).astype(jnp.bfloat16)
    returned = lax.all_to_all(
        partial_out.reshape(arrived_rows.shape),
        ("dp", "ep"),
        split_axis=0,
        concat_axis=0,
        tiled=True,
    )
    expert_out = jnp.sum(
        returned.reshape(dp_count, ep_count, capacity, model_width).astype(jnp.float32), axis=0
    ).astype(jnp.bfloat16)
    routed = jnp.einsum(
        "rec,ecd->rd", combining, expert_out.astype(jnp.float32), precision=lax.Precision.HIGHEST
    )
    return (widened + routed).astype(jnp.bfloat16)


def solution(mesh):
    placed = (
        P(("dp", "ep"), None),
        P(("dp", "ep"), None, None),
        P(("dp", "ep"), None, None),
        P(("dp", "ep"), None, None),
        P(("dp", "ep"), None, None),
        P(("dp", "ep"), None),
        P(("dp", "ep")),
        P(("dp", "ep")),
        P(("dp", "ep")),
        P(("dp", "ep"), None),
        P(("dp", "ep"), None),
        P(),
        P("ep", None, None),
        P("ep", None),
        P("ep", None, "dp"),
        P("ep", None, "dp"),
        P("ep", "dp", None),
    )
    return jax.shard_map(
        on_device, mesh=mesh, in_specs=placed, out_specs=P(("dp", "ep"), None), check_vma=False
    )
```

profile of v0, /device:TPU:1, one launch (start us, length us, event | category | flops | bytes accessed | tf_op | source)
XLA Modules:
  0.0 285.0 jit_solution(3642160557098070118)
XLA Ops:
  6.5 0.8 compare_select_fusion
  7.3 0.1 reshape.139
  7.4 1.1 reshape.130
  8.6 0.6 gather_fusion
  9.2 1.3 gather_fusion.1
  10.6 0.1 iota_compare_fusion.2
  10.6 1.5 fusion.49
  12.1 1.4 fusion.48
  13.5 0.2 fusion.21
  13.7 0.5 fusion.13
  14.2 0.1 copy.45
  14.3 15.3 %all_to_all.34 = bf16[2,64,512]{2,0,1:T(2,128)(2,1)S(1)} all-to-all(bf16[2,64,512]{2,0,1:T(2,128)(2,1)S(1)} %copy.45), channel_id=1, replica_groups=mesh['dp'=8,'ep'=16] {'ep'}, dimensions={1} | all-to-all | bytes 262144 | tf_op jit(solution)/shard_map/all_to_all | solution.py:80
  29.6 0.1 copy.64
  29.7 0.1 all_to_all.26
  29.8 1.2 fusion.19
  31.0 0.0 copy-start.3
  31.0 0.0 copy-start.6
  31.0 0.0 copy-start.1
  31.0 0.0 copy-start.2
  31.0 5.3 %convolution_convert_fusion.2 = bf16[32,7168]{1,0:T(8,128)(2,1)} fusion(bf16[512,7168]{1,0:T(8,128)(2,1)} %param.30, bf16[4,4,8,128]{3,2,1,0:T(8,128)(2,1)S(1)} %fusion.19), kind=kOutput, calls=%fused_computation.4 | convolution fusion | flops 235110400 | bytes 7831552 | tf_op jit(solution)/shard_map/dot_general | solution.py:86
  36.3 0.0 all-reduce.3.cloned.1.call-update
  37.7 0.1 convert_reduce_fusion
  37.8 0.6 dynamic-slice
  39.1 79.7 %all-reduce.3.cloned.1.call-done = bf16[32,7168]{1,0:T(8,128)(2,1)} async-done(((bf16[32,7168]{1,0:T(8,128)(2,1)}), bf16[32,7168]{1,0:T(8,128)(2,1)}) %all-reduce.3.cloned.1.call-update) | async-done | bytes 458768
  118.8 0.9 add_convert_fusion
  119.7 0.1 dynamic-slice_reduce_fusion
  119.8 0.2 broadcast_select_fusion
  120.1 0.5 broadcast.130
  120.6 1.3 reduce.5
  121.9 0.7 reshape.165
  122.6 6.3 %all-to-all-start.1 = ((bf16[8,2,3584]{2,1,0:T(2,128)(2,1)}), bf16[8,2,3584]{2,1,0:T(2,128)(2,1)S(1)}, u32[]{:S(2)}, u32[]{:S(2)}) async-start(bf16[8,2,3584]{2,1,0:T(2,128)(2,1)} %reshape.165), calls=%async_computation.1 | async-start | bytes 229376 | tf_op jit(solution)/shard_map/all_to_all | solution.py:93
  128.9 5.1 %all-to-all-done.1 = bf16[8,2,3584]{2,1,0:T(2,128)(2,1)S(1)} async-done(((bf16[8,2,3584]{2,1,0:T(2,128)(2,1)}), bf16[8,2,3584]{2,1,0:T(2,128)(2,1)S(1)}, u32[]{:S(2)}, u32[]{:S(2)}) %all-to-all-start.1) | async-done | bytes 114720 | tf_op jit(solution)/shard_map/all_to_all | solution.py:93
  134.0 0.1 reshape.166
  134.1 0.2 reduce_sum.52
  134.3 0.3 fusion.31
  134.6 0.3 convolution_convert_fusion.1
  134.9 0.5 copy.49
  135.4 1.9 broadcast_in_dim.85
  137.3 51.9 %all_to_all.35 = bf16[128,2,7168]{2,1,0:T(2,128)(2,1)} all-to-all(bf16[128,2,7168]{2,1,0:T(2,128)(2,1)S(1)} %bitcast.66), channel_id=1, replica_groups=mesh['dp'=8,'ep'=16] {'dp','ep'}, dimensions={0} | all-to-all | bytes 7340032 | tf_op jit(solution)/shard_map/all_to_all | solution.py:118
  189.2 8.4 %reshape.134 = bf16[256,7168]{1,0:T(8,128)(2,1)} reshape(bf16[128,2,7168]{2,1,0:T(2,128)(2,1)} %all_to_all.35) | data formatting | bytes 7340032 | tf_op jit(solution)/shard_map/reshape | solution.py:119
  197.6 4.3 %fusion.5 = f32[256,256]{1,0:T(8,128)S(1)} fusion(bf16[256,7168]{1,0:T(8,128)(2,1)} %reshape.134, bf16[1,7168,256]{2,1,0:T(8,128)(2,1)} %param.31), kind=kOutput, calls=%fused_computation.11 | convolution fusion | flops 939524096 | bytes 7602176 | tf_op jit(solution)/shard_map/dot_general | solution.py:120
  201.8 10.0 %convolution_convert_fusion = bf16[256,7168]{1,0:T(8,128)(2,1)} fusion(bf16[1,256,7168]{2,1,0:T(8,128)(2,1)} %param.33, bf16[256,7168]{1,0:T(8,128)(2,1)} %reshape.134, bf16[1,7168,256]{2,1,0:T(8,128)(2,1)} %param.32, f32[256,256]{1,0:T(8,128)S(1)} %fusion.5), kind=kOutput, calls=%fused_computation.2 | convolution fusion | flops 1881276416 | bytes 14942208 | tf_op jit(solution)/shard_map/dot_general | solution.py:123
  211.9 8.1 %reshape.135 = bf16[128,2,7168]{2,1,0:T(2,128)(2,1)} reshape(bf16[256,7168]{1,0:T(8,128)(2,1)} %convolution_convert_fusion) | data formatting | bytes 7340032 | tf_op jit(solution)/shard_map/reshape | solution.py:125
  220.0 5.6 %all-to-all-start.3 = ((bf16[128,2,7168]{2,1,0:T(2,128)(2,1)}), bf16[128,2,7168]{2,1,0:T(2,128)(2,1)}, u32[]{:S(2)}, u32[]{:S(2)}) async-start(bf16[128,2,7168]{2,1,0:T(2,128)(2,1)} %reshape.135), calls=%async_computation.3 | async-start | bytes 7340032 | tf_op jit(solution)/shard_map/all_to_all | solution.py:124
  225.6 0.2 fusion.38
  225.8 45.7 %all-to-all-done.3 = bf16[128,2,7168]{2,1,0:T(2,128)(2,1)} async-done(((bf16[128,2,7168]{2,1,0:T(2,128)(2,1)}), bf16[128,2,7168]{2,1,0:T(2,128)(2,1)}, u32[]{:S(2)}, u32[]{:S(2)}) %all-to-all-start.3) | async-done | bytes 3670048 | tf_op jit(solution)/shard_map/all_to_all | solution.py:124
  271.5 5.7 %reduce_sum.55 = bf16[16,2,7168]{2,1,0:T(2,128)(2,1)S(1)} reduce(bf16[8,16,2,7168]{3,2,1,0:T(2,128)(2,1)} %bitcast.17, bf16[]{:T(256)} %constant.29.clone.1), dimensions={0}, to_apply=%region_7.8 | reduce | flops 1605632 | bytes 4128770 | tf_op jit(solution)/shard_map/reduce_sum | solution.py:131
  277.2 1.0 fusion.1
  (18 shorter events, 0.1 us)
Async XLA Ops:
  6.5 2.0 copy-start
  6.5 4.0 %copy-start.4 = (s32[2]{0:T(128)S(1)}, s32[2]{0:T(128)}, u32[]{:S(2)}) copy-start(s32[2]{0:T(128)} %param.23) | copy-start | bytes 28
  6.5 112.2 %all-reduce.3.cloned.1.call-start = ((), (), s32[]{:S(2)}) async-start(), calls=%async_computation.4 | async-start | bytes 917504
  31.0 6.7 %copy-start.3 = (s32[2,8]{1,0:T(2,128)S(1)}, s32[2,8]{1,0:T(2,128)}, u32[]{:S(2)}) copy-start(s32[2,8]{1,0:T(2,128)} %param.26) | copy-start | bytes 196
  31.0 6.8 %copy-start.6 = (u32[128]{0:T(128)S(1)}, u32[128]{0:T(128)}, u32[]{:S(2)}) copy-start(u32[128]{0:T(128)} %constant.50) | copy-start | bytes 1540
  31.0 87.8 %copy-start.1 = (bf16[2,7168]{1,0:T(2,128)(2,1)S(1)}, bf16[2,7168]{1,0:T(2,128)(2,1)}, u32[]{:S(2)}) copy-start(bf16[2,7168]{1,0:T(2,128)(2,1)} %param.17) | copy-start | bytes 86020
  31.0 103.5 %copy-start.2 = (f32[7168]{0:T(1024)S(1)}, f32[7168]{0:T(1024)}, u32[]{:S(2)}) copy-start(f32[7168]{0:T(1024)} %param.28) | copy-start | bytes 86020
  122.6 11.4 %all-to-all-start.1 = ((bf16[8,2,3584]{2,1,0:T(2,128)(2,1)}), bf16[8,2,3584]{2,1,0:T(2,128)(2,1)S(1)}, u32[]{:S(2)}, u32[]{:S(2)}) async-start(bf16[8,2,3584]{2,1,0:T(2,128)(2,1)} %reshape.165), calls=%async_computation.1 | async-start | bytes 229376 | tf_op jit(solution)/shard_map/all_to_all | solution.py:93
  220.0 5.6 %copy-start.5 = (f32[2,8]{1,0:T(2,128)S(1)}, f32[2,8]{1,0:T(2,128)}, u32[]{:S(2)}) copy-start(f32[2,8]{1,0:T(2,128)} %param.27) | copy-start | bytes 196
  220.0 51.5 %all-to-all-start.3 = ((bf16[128,2,7168]{2,1,0:T(2,128)(2,1)}), bf16[128,2,7168]{2,1,0:T(2,128)(2,1)}, u32[]{:S(2)}, u32[]{:S(2)}) async-start(bf16[128,2,7168]{2,1,0:T(2,128)(2,1)} %reshape.135), calls=%async_computation.3 | async-start | bytes 7340032 | tf_op jit(solution)/shard_map/all_to_all | solution.py:124
Sparse Core Ops, SparseCore 0:
  36.5 82.2 all-reduce.2
where the time goes:
time: 286 us; the launch traced here: 285 us
  waiting for transfers between devices  131 us (46%)
  blocking collectives  67.1 us (23%)
  matrix products  25.7 us (9%)
  local copies, waits for them, and re-layouts  24.4 us (9%)
  between operations  15.6 us (5%)
  starting transfers between devices  11.9 us (4%)
  other arithmetic  9.88 us (3%)
    unnamed x2, waiting for transfers between devices  79.7 us
    all_to_all x1, blocking collectives, on_device(): lax.all_to_all(spread, ('dp', 'ep'), split_axis=0, concat_axis=0, tiled=T...  51.9 us
    all_to_all x1, waiting for transfers between devices, on_device(): lax.all_to_all(partial_out.reshape(arrived_rows.shape), ('dp', 'ep'), spl...  45.7 us
    all_to_all x1, blocking collectives, on_device(): lax.all_to_all(latent_out, 'ep', split_axis=1, concat_axis=0, tiled=True)  15.3 us
    dot_general x1, matrix products, on_device(): jnp.dot(inner, w_down[0], preferred_element_type=jnp.float32)  10 us
    reshape x1, local copies, waits for them, and re-layouts, on_device(): flat_rows = arrived_rows.reshape(-1, model_width)  8.4 us
    reshape x1, local copies, waits for them, and re-layouts, on_device(): partial_out.reshape(arrived_rows.shape)  8.12 us
    all_to_all x1, starting transfers between devices, on_device(): lax.all_to_all(row_parcel, 'dp', split_axis=0, concat_axis=0, tiled=True)  6.29 us
  transfers between devices with their start and end apart: 3, of which 3 were waited for; matrix products, arithmetic and copies ran while one was open for 0% of the time, Pallas kernels for 0%

commit v1 on v0

v1 whole, which is shorter than its diff:
```python
import functools

import jax
import jax.numpy as jnp
from jax import lax
from jax.experimental import pallas as pl
from jax.experimental.pallas import tpu as pltpu
from jax.sharding import PartitionSpec as P

MESH = pl.DeviceIdType.MESH
BF = jnp.bfloat16
F32 = jnp.float32

D = 7168
HALF = D // 2
BLK = 896
PIECES = (384, 256, 256)
STARTS = (0, 384, 640)
GATHER = (("y", "z", "x"), ("z", "x", "y"), ("x", "y", "z"))
REDUCE = (("x", "y", "z"), ("y", "z", "x"), ("z", "x", "y"))
BASE = (0, 5, 10)
COUNT = (5, 5, 4)
CHUNKS = [(p, q) for q in range(5) for p in range(3) if q < COUNT[p]]

SCRATCH = dict(
    qv=pltpu.VMEM((2, 64, 512), BF),
    qrv=pltpu.VMEM((2, 64, 64), BF),
    pgv=pltpu.VMEM((24, 64, 512), BF),
    rpv=pltpu.VMEM((24, 32, 128), BF),
    uvv=pltpu.VMEM((4, 512, 128), BF),
    wov=pltpu.VMEM((8, 512, BLK), BF),
    wv=pltpu.VMEM((4, HALF, 256), BF),
    wd=pltpu.VMEM((2, 256, HALF), BF),
    scores=pltpu.VMEM((6, 128, 256), F32),
    a_send=pltpu.VMEM((16, 16, 256), BF),
    a_recv=pltpu.VMEM((16, 16, 256), BF),
    r_send=pltpu.VMEM((8, 2, 16, BLK), BF),
    r_recv=pltpu.VMEM((16, 16, BLK), BF),
    m_one=pltpu.VMEM((16, 8, 128), F32),
    m_all=pltpu.VMEM((8, 16, 128), F32),
    xa=pltpu.VMEM((4, 4, 4, 16, PIECES[0]), BF),
    xb=pltpu.VMEM((4, 4, 4, 16, PIECES[1]), BF),
    xc=pltpu.VMEM((4, 4, 4, 16, PIECES[2]), BF),
    xg=pltpu.VMEM((256, BLK), BF),
    pre=pltpu.VMEM((4, 256, 256), F32),
    squares=pltpu.VMEM((256, 128), F32),
    squares_in=pltpu.VMEM((256, 128), F32),
    pre_send=pltpu.VMEM((4, 256, 256), BF),
    pre_recv=pltpu.VMEM((4, 256, 256), BF),
    inner=pltpu.VMEM((2, 256, 256), BF),
    sorted_in=pltpu.VMEM((3, 2, 256, 256), BF),
    perm=pltpu.VMEM((3, 256, 256), BF),
    weight=pltpu.VMEM((3, 256, 128), F32),
    resid=pltpu.VMEM((16, HALF), F32),
    c_send=pltpu.VMEM((14, 4, 64, 256), BF),
    c_recv=pltpu.VMEM((14, 4, 64, 256), BF),
    b_send=pltpu.VMEM((14, 4, 16, 256), BF),
    b_recv=pltpu.VMEM((14, 4, 16, 256), BF),
    f_send=pltpu.VMEM((3, 8, 2, 1280), F32),
    f_recv=pltpu.VMEM((3, 8, 2, 1280), F32),
    load_sem=pltpu.SemaphoreType.DMA((16,)),
    swap_s=pltpu.SemaphoreType.DMA((8,)),
    swap_r=pltpu.SemaphoreType.DMA((8,)),
    a_s=pltpu.SemaphoreType.DMA((16,)),
    a_r=pltpu.SemaphoreType.DMA((16,)),
    r_s=pltpu.SemaphoreType.DMA((16,)),
    r_r=pltpu.SemaphoreType.DMA((16,)),
    m_s=pltpu.SemaphoreType.DMA((16,)),
    m_r=pltpu.SemaphoreType.DMA((16,)),
    n_s=pltpu.SemaphoreType.DMA((8,)),
    n_r=pltpu.SemaphoreType.DMA((8,)),
    g_s=pltpu.SemaphoreType.DMA((2, 3, 4)),
    g_r=pltpu.SemaphoreType.DMA((2, 3, 4)),
    h_s=pltpu.SemaphoreType.DMA((3, 4, 4)),
    h_r=pltpu.SemaphoreType.DMA((3, 4, 4)),
    c_s=pltpu.SemaphoreType.DMA((14, 4)),
    c_r=pltpu.SemaphoreType.DMA((14, 4)),
    b_s=pltpu.SemaphoreType.DMA((14, 4)),
    b_r=pltpu.SemaphoreType.DMA((14, 4)),
    f_s=pltpu.SemaphoreType.DMA((3, 8)),
    f_r=pltpu.SemaphoreType.DMA((3, 8)),
)


def iota(shape, dim):
    return lax.broadcasted_iota(jnp.int32, shape, dim)


def ones_where(mask):
    return jnp.where(mask, 1.0, 0.0).astype(BF)


def dot(a, b):
    return jnp.dot(a, b, preferred_element_type=F32)


def dot_nt(a, b):
    return lax.dot_general(a, b, (((1,), (1,)), ((), ())), preferred_element_type=F32)


def layer(
    hidden,
    gain,
    table,
    lens,
    move_req,
    move_to,
    routing,
    gates,
    q_latent,
    q_rope,
    pages,
    ropes,
    w_uv,
    w_out,
    w_gate,
    w_up,
    w_down,
    out,
    *scratch,
):
    s = dict(zip(SCRATCH, scratch))
    i = lax.axis_index("dp")
    j = lax.axis_index("ep")
    x, c = lax.div(i, 2), lax.rem(i, 2)
    z, y = lax.div(j, 4), lax.rem(j, 4)
    other = 1 - c
    at = {"x": x, "y": y, "z": z}

    def place(axis, value, core):
        if axis == "x":
            return (value * 2 + core, j)
        if axis == "y":
            return (x * 2 + core, z * 4 + value)
        return (x * 2 + core, value * 4 + y)

    def turn(axis, k):
        return lax.rem(at[axis] + k, 4)

    def remote(src, dst, send, recv, device):
        return pltpu.make_async_remote_copy(
            src_ref=src, dst_ref=dst, send_sem=send, recv_sem=recv, device_id=device, device_id_type=MESH
        )

    sibling = (x * 2 + other, j)

    barrier = pltpu.get_barrier_semaphore()

    def greet(m, carry):
        t = lax.rem(c * 16 + j + m, 32)
        pl.semaphore_signal(
            barrier, inc=1, device_id=(x * 2 + lax.div(t, 16), lax.rem(t, 16)), device_id_type=MESH
        )
        return carry

    lax.fori_loop(1, 32, greet, 0)
    for k in (1, 2, 3):
        for core in (0, 1):
            pl.semaphore_signal(barrier, inc=1, device_id=place("x", turn("x", k), core), device_id_type=MESH)

    half = pl.multiple_of(c * HALF, 128)
    others = pl.multiple_of(other * HALF, 128)
    loads = [
        (q_latent, s["qv"]),
        (q_rope, s["qrv"]),
        (ropes, s["rpv"]),
        (pages, s["pgv"]),
        (w_uv, s["uvv"]),
    ]
    loads += [(w_out.at[:, pl.ds(n * BLK, BLK)], s["wov"].at[n]) for n in range(8)]
    loads += [
        (w_gate.at[0, pl.ds(half, HALF), :], s["wv"].at[0]),
        (w_up.at[0, pl.ds(half, HALF), :], s["wv"].at[1]),
        (w_down.at[0, :, pl.ds(half, HALF)], s["wd"].at[0]),
    ]
    loads = [pltpu.make_async_copy(src, dst, s["load_sem"].at[n]) for n, (src, dst) in enumerate(loads)]
    for load in loads:
        load.start()

    row = iota((128, 128), 0)
    col = iota((128, 128), 1)
    wanted = lax.rem(lax.div(row, 4), 2) * 64 + lax.div(row, 8) * 4 + lax.rem(row, 4)
    order = ones_where(col == wanted)
    twice = ones_where(iota((64, 128), 0) == lax.rem(iota((64, 128), 1), 64))
    first_row = lax.rem(lax.div(iota((128, 1), 0), 4), 2) == 0
    spread = ones_where(lax.div(iota((256, 128), 0), 2) == iota((256, 128), 1))
    parity = lax.div(iota((256, 128), 1), 64) == lax.rem(iota((256, 128), 0), 2)
    place_of = iota((1, 1536), 1)
    bias = []
    for r in range(2):
        live = jnp.zeros((1, 1536), jnp.int32)
        for q in range(12):
            start = table[r, q] * 64
            count = jnp.clip(lens[r] - q * 64, 0, 64)
            live = jnp.where((place_of >= start) & (place_of < start + count), 1, live)
        bias.append(jnp.where(live > 0, 0.0, -1e30))
    scale = 192.0 ** (-0.5)
    loads[0].wait()
    loads[1].wait()
    query = dot(order, s["qv"][...].reshape(128, 512)).astype(BF)
    rotary = dot(dot(order, s["qrv"][...].reshape(128, 64)).astype(BF), twice).astype(BF)
    loads[2].wait()
    loads[3].wait()
    largest = jnp.full((128, 1), -1e30, F32)
    for n in range(6):
        keys = s["pgv"][4 * n : 4 * n + 4].reshape(256, 512)
        turned = dot(spread, s["rpv"][4 * n : 4 * n + 4].reshape(128, 128))
        turned = jnp.where(parity, turned, 0.0).astype(BF)
        score = (dot_nt(query, keys) + dot_nt(rotary, turned)) * scale
        cut = slice(256 * n, 256 * n + 256)
        score = score + jnp.where(first_row, bias[0][:, cut], bias[1][:, cut])
        s["scores"][n] = score
        largest = jnp.maximum(largest, jnp.max(score, axis=1, keepdims=True))
    total = jnp.zeros((128, 1), F32)
    mixed = jnp.zeros((128, 512), F32)
    for n in range(6):
        prob = jnp.exp(s["scores"][n] - largest)
        total = total + jnp.sum(prob, axis=1, keepdims=True)
        mixed = mixed + dot(prob.astype(BF), s["pgv"][4 * n : 4 * n + 4].reshape(256, 512))
    mixed = mixed / total
    lower = mixed[:, :256].reshape(16, 8, 256)
    upper = mixed[:, 256:].reshape(16, 8, 256)
    s["a_send"][...] = jnp.concatenate([lower, upper], axis=1).astype(BF)
    s["a_recv"][j] = s["a_send"][j]

    pl.semaphore_wait(barrier, 37)

    def a_copy(k, land):
        t = lax.rem(j + k, 16)
        return remote(s["a_send"].at[t], s["a_recv"].at[land], s["a_s"].at[k], s["a_r"].at[k], (i, t))

    def a_start(k, carry):
        a_copy(k, j).start()
        return carry

    lax.fori_loop(1, 16, a_start, 0)

    lane = iota((8, 128), 1)
    note = jnp.zeros((8, 128), F32)
    for r in range(2):
        for k in range(8):
            note = jnp.where(lane == routing[r, k] + 16 * r, gates[r, k], note)
    note = jnp.where(lane == 32, move_req[0].astype(F32), note)
    note = jnp.where(lane == 33, move_to[0].astype(F32), note)
    s["m_one"][j] = jnp.where(iota((8, 128), 0) == 0, note, 0.0)

    def m_copy(k, land):
        t = lax.rem(j + k, 16)
        return remote(s["m_one"].at[land], s["m_one"].at[land], s["m_s"].at[k], s["m_r"].at[k], (i, t))

    def m_start(k, carry):
        m_copy(k, j).start()
        return carry

    lax.fori_loop(1, 16, m_start, 0)

    swaps = [
        (w_gate.at[0, pl.ds(others, HALF), :], s["wv"].at[2]),
        (w_up.at[0, pl.ds(others, HALF), :], s["wv"].at[3]),
        (w_down.at[0, :, pl.ds(others, HALF)], s["wd"].at[1]),
    ]
    swaps = [remote(a, b, s["swap_s"].at[n], s["swap_r"].at[n], sibling) for n, (a, b) in enumerate(swaps)]
    for swap in swaps:
        swap.start()

    def a_wait(k, carry):
        a_copy(k, lax.rem(j + 16 - k, 16)).wait_recv()
        return carry

    target = iota((256, 256), 0)
    inside = lax.rem(target, 128)
    wanted = (
        lax.div(lax.rem(inside, 32), 2) * 16
        + lax.div(target, 128) * 8
        + lax.rem(inside, 2) * 4
        + lax.div(inside, 32)
    )
    by_head = ones_where(iota((256, 256), 1) == wanted)
    loads[4].wait()
    lax.fori_loop(1, 16, a_wait, 0)
    grouped = dot(by_head, s["a_recv"][...].reshape(256, 256)).astype(BF)
    values = []
    for h in range(4):
        low = grouped[32 * h : 32 * h + 32]
        high = grouped[128 + 32 * h : 160 + 32 * h]
        values.append((dot(low, s["uvv"][h, :256]) + dot(high, s["uvv"][h, 256:])).astype(BF))
    values = jnp.concatenate(values, axis=1)
    for n in range(8):
        loads[5 + n].wait()
    request = iota((32, 1), 0)

    def r_target(n, h):
        core, zz = lax.div(n, 4), lax.rem(n, 4)
        return core, zz, 2 * c + h

    def r_copy(n, h):
        core, zz, yy = r_target(n, h)
        m = n * 2 + h
        return remote(
            s["r_send"].at[n, h],
            s["r_recv"].at[j],
            s["r_s"].at[m],
            s["r_r"].at[j],
            (x * 2 + core, zz * 4 + yy),
        )

    def r_mine(n, h):
        core, zz, yy = r_target(n, h)
        return (core == c) & (zz == z) & (yy == y)

    def r_start(n, carry):
        width = pl.multiple_of(n * BLK, 128)
        part = dot(values, s["wov"][n])
        own = hidden[:, pl.ds(width, BLK)].astype(F32)
        part = part + jnp.where(
            request == 2 * j, own[0:1], jnp.where(request == 2 * j + 1, own[1:2], 0.0)
        )
        s["r_send"][n] = part.astype(BF).reshape(2, 16, BLK)
        for h in range(2):

            @pl.when(jnp.logical_not(r_mine(n, h)))
            def _():
                r_copy(n, h).start()

            @pl.when(r_mine(n, h))
            def _():
                s["r_recv"][j] = s["r_send"][n, h]

        return carry

    lax.fori_loop(0, 8, r_start, 0)

    def m_wait(k, carry):
        m_copy(k, lax.rem(j + 16 - k, 16)).wait_recv()
        return carry

    lax.fori_loop(1, 16, m_wait, 0)
    s["m_all"][i] = jnp.sum(s["m_one"][...], axis=1)

    def n_copy(k, land):
        t = lax.rem(i + k, 8)
        return remote(s["m_all"].at[land], s["m_all"].at[land], s["n_s"].at[k], s["n_r"].at[k], (t, j))

    def n_start(k, carry):
        n_copy(k, i).start()
        return carry

    lax.fori_loop(1, 8, n_start, 0)

    def r_wait(t, carry):
        @pl.when(jnp.logical_not((lax.div(y, 2) == c) & (t == j)))
        def _():
            remote(s["r_send"].at[0, 0], s["r_recv"].at[t], s["r_s"].at[0], s["r_r"].at[t], sibling).wait_recv()

        return carry

    lax.fori_loop(0, 16, r_wait, 0)
    block = jnp.zeros((16, BLK), F32)
    for t in range(16):
        block = block + s["r_recv"][t].astype(F32)
    block = block.astype(BF)
    pieces = (s["xa"], s["xb"], s["xc"])
    for p in range(3):
        pieces[p][z, x, y] = block[:, STARTS[p] : STARTS[p] + PIECES[p]]

    def view(p, whole, fixed):
        where = [slice(None) if a in whole else fixed.get(a, at[a]) for a in ("z", "x", "y")]
        return pieces[p].at[tuple(where)]

    def g_copy(step, p, k, landing):
        axis = GATHER[p][step]
        fixed = {axis: turn(axis, 4 - k)} if landing else {}
        ref = view(p, GATHER[p][:step], fixed)
        return remote(
            ref, ref, s["g_s"].at[step, p, k], s["g_r"].at[step, p, k], place(axis, turn(axis, k), c)
        )

    def h_copy(p, kk, k, landing):
        axis = GATHER[p][2]
        fixed = {axis: turn(axis, 4 - k)} if landing else {}
        if axis != "z":
            fixed["z"] = turn("z", kk)
        ref = view(p, [a for a in ("x", "y") if a != axis], fixed)
        return remote(ref, ref, s["h_s"].at[p, kk, k], s["h_r"].at[p, kk, k], place(axis, turn(axis, k), c))

    for step in range(2):
        for p in range(3):
            if step:
                for k in (1, 2, 3):
                    g_copy(step - 1, p, k, True).wait_recv()
            for k in (1, 2, 3):
                g_copy(step, p, k, False).start()
    for p in (2, 0, 1):
        for k in (1, 2, 3):
            g_copy(1, p, k, True).wait_recv()
        for kk in range(4 if p < 2 else 1):
            for k in (1, 2, 3):
                h_copy(p, kk, k, False).start()

    def n_wait(k, carry):
        n_copy(k, lax.rem(i + 8 - k, 8)).wait_recv()
        return carry

    lax.fori_loop(1, 8, n_wait, 0)
    notes = s["m_all"][...].reshape(128, 128)
    notes_high = notes.astype(BF)
    notes_low = (notes - notes_high.astype(F32)).astype(BF)
    picked = dot_nt(ones_where(iota((8, 128), 1) == 32 + iota((8, 128), 0)), notes_high).astype(BF)
    picked = dot(picked, ones_where(lax.div(iota((128, 256), 1), 2) == iota((128, 256), 0)))
    home = iota((1, 256), 1)
    home_key = jnp.where(
        picked[0:1] == lax.rem(home, 2).astype(F32),
        256.0 + picked[1:2] * 16.0 + lax.rem(lax.div(home, 2), 16).astype(F32),
        home.astype(F32),
    )

    def arrange(device, slot):
        size = device.shape[0]
        lanes = iota((size, 128), 1)
        found = ones_where(lanes == device)
        found = dot(found, notes_high) + dot(found, notes_low)
        weigh = jnp.sum(jnp.where(lanes == slot * 16 + j, found, 0.0), axis=1, keepdims=True)
        leaving = jnp.sum(jnp.where(lanes == 32, found, 0.0), axis=1, keepdims=True)
        key = jnp.where(
            leaving == slot.astype(F32), 256.0 + device.astype(F32), (2 * device + slot).astype(F32)
        )
        return ones_where(key == home_key), weigh

    t = iota((256, 1), 0)
    for p in range(3):
        coords = {
            REDUCE[p][0]: lax.div(t, 64),
            REDUCE[p][1]: lax.rem(lax.div(t, 16), 4),
            REDUCE[p][2]: lax.rem(lax.div(t, 4), 4),
        }
        device = (coords["x"] * 2 + lax.rem(lax.div(t, 2), 2)) * 16 + coords["z"] * 4 + coords["y"]
        matrix, weigh = arrange(device, lax.rem(t, 2))
        s["perm"][p] = matrix
        s["weight"][p] = jnp.broadcast_to(weigh, (256, 128))
    t = iota((16, 1), 0)
    chosen, _ = arrange((x * 2 + lax.rem(lax.div(t, 2), 2)) * 16 + j, lax.rem(t, 2))

    for n in range(13, 15):
        loads[n].wait()
    for n in range(2):
        swaps[n].wait_recv()
    s["pre"][...] = jnp.zeros((4, 256, 256), F32)
    s["squares"][...] = jnp.zeros((256, 128), F32)

    def project(kk, carry):
        zz = turn("z", kk)
        for p in range(2):
            for k in (1, 2, 3):
                h_copy(p, kk, k, True).wait_recv()

        @pl.when(kk > 0)
        def _():
            h_copy(2, 0, 4 - kk, True).wait_recv()

        squares = s["squares"][...]
        for p in range(3):
            rows = pieces[p][zz].reshape(256, PIECES[p]).astype(F32)
            for n in range(PIECES[p] // 128):
                tile = rows[:, 128 * n : 128 * n + 128]
                squares = squares + tile * tile
            width = pl.multiple_of(c * HALF + zz * BLK + STARTS[p], 128)
            s["xg"][:, STARTS[p] : STARTS[p] + PIECES[p]] = (
                rows * gain[:, pl.ds(width, PIECES[p])]
            ).astype(BF)
        s["squares"][...] = squares
        depth = pl.multiple_of(zz * BLK, 128)
        for m in range(4):
            s["pre"][m] = s["pre"][m] + dot(s["xg"][...], s["wv"][m, pl.ds(depth, BLK), :])
        return carry

    lax.fori_loop(0, 4, project, 0)

    halves = [
        remote(s["pre_send"].at[m], s["pre_recv"].at[(m + 2) % 4], s["swap_s"].at[3 + m], s["swap_r"].at[3 + (m + 2) % 4], sibling)
        for m in range(4)
    ]
    sums = remote(s["squares"], s["squares_in"], s["swap_s"].at[7], s["swap_r"].at[7], sibling)
    sums.start()
    for m in (2, 3, 0, 1):
        s["pre_send"][m] = s["pre"][m].astype(BF)
        halves[m].start()
    sums.wait_recv()
    square = jnp.sum(s["squares"][...] + s["squares_in"][...], axis=1, keepdims=True)
    norm = lax.rsqrt(square / D + 1e-06)
    for b in range(2):
        halves[(2 * b + 2) % 4].wait_recv()
        halves[(2 * b + 3) % 4].wait_recv()
        gate = (s["pre"][2 * b] + s["pre_recv"][2 * b].astype(F32)) * norm
        up = (s["pre"][2 * b + 1] + s["pre_recv"][2 * b + 1].astype(F32)) * norm
        s["inner"][b] = (gate / (1.0 + jnp.exp(-gate)) * up).astype(BF)
    for p in range(3):
        weigh = s["weight"][p][:, 0:1]
        for b in range(2):
            s["sorted_in"][p, b] = (dot(s["perm"][p], s["inner"][b]) * weigh).astype(BF)

    def c_copy(n, p, k, landing):
        axis = REDUCE[p][0]
        return remote(
            s["c_send"].at[n, turn(axis, k)],
            s["c_recv"].at[n, k],
            s["c_s"].at[n, k],
            s["c_r"].at[n, k],
            place(axis, turn(axis, k), c),
        )

    def b_copy(n, p, k, landing):
        axis = REDUCE[p][1]
        return remote(
            s["b_send"].at[n, turn(axis, k)],
            s["b_recv"].at[n, k],
            s["b_s"].at[n, k],
            s["b_r"].at[n, k],
            place(axis, turn(axis, k), c),
        )

    loads[15].wait()
    swaps[2].wait_recv()
    for p, q in CHUNKS:
        n = BASE[p] + q
        cols = slice(256 * n, 256 * n + 256)
        part = dot(s["sorted_in"][p, 0], s["wd"][0, :, cols]) + dot(s["sorted_in"][p, 1], s["wd"][1, :, cols])
        s["c_send"][n] = part.astype(BF).reshape(4, 64, 256)
        for k in (1, 2, 3):
            c_copy(n, p, k, False).start()

    for p in range(3):
        for zz in range(4):
            begin = zz * BLK + STARTS[p]
            s["resid"][:, begin : begin + PIECES[p]] = dot(chosen, pieces[p][zz].reshape(256, PIECES[p]))

    for p, q in CHUNKS:
        n = BASE[p] + q
        axis = REDUCE[p][0]
        for k in (1, 2, 3):
            c_copy(n, p, k, True).wait_recv()
        part = s["c_send"][n, at[axis]].astype(F32)
        for k in (1, 2, 3):
            part = part + s["c_recv"][n, k].astype(F32)
        s["b_send"][n] = part.astype(BF).reshape(4, 16, 256)
        for k in (1, 2, 3):
            b_copy(n, p, k, False).start()

    def f_copy(p, m, landing):
        axis = REDUCE[p][2]
        mine = at[axis] * 2 + c
        t = lax.rem(mine + m, 8)
        wide = pl.ds(0, COUNT[p] * 256)
        land = lax.rem(mine + 8 - m, 8) if landing else mine
        return remote(
            s["f_send"].at[p, t, :, wide],
            s["f_recv"].at[p, land, :, wide],
            s["f_s"].at[p, m],
            s["f_r"].at[p, m],
            place(axis, lax.div(t, 2), lax.rem(t, 2)),
        )

    last = lax.div(iota((16, 1), 0), 4)
    for p, q in CHUNKS:
        n = BASE[p] + q
        for k in (1, 2, 3):
            b_copy(n, p, k, True).wait_recv()
        part = s["b_send"][n, at[REDUCE[p][1]]].astype(F32)
        for k in (1, 2, 3):
            part = part + s["b_recv"][n, k].astype(F32)
        part = part + jnp.where(last == at[REDUCE[p][2]], s["resid"][:, 256 * n : 256 * n + 256], 0.0)
        for t in range(8):
            s["f_send"][p, t, :, 256 * q : 256 * q + 256] = part[2 * t : 2 * t + 2]
        if q == COUNT[p] - 1:
            for m in range(1, 8):
                f_copy(p, m, False).start()
            mine = at[REDUCE[p][2]] * 2 + c
            s["f_recv"][p, mine] = s["f_send"][p, mine]
    for p in (2, 0, 1):
        for m in range(1, 8):
            f_copy(p, m, True).wait_recv()
        for core in range(2):
            part = s["f_recv"][p, core]
            for t in range(1, 4):
                part = part + s["f_recv"][p, 2 * t + core]
            wide = COUNT[p] * 256
            begin = core * HALF + BASE[p] * 256
            out[:, begin : begin + wide] = part[:, :wide].astype(BF)

    def a_done(k, carry):
        a_copy(k, j).wait_send()
        m_copy(k, j).wait_send()
        return carry

    lax.fori_loop(1, 16, a_done, 0)

    def n_done(k, carry):
        n_copy(k, i).wait_send()
        return carry

    lax.fori_loop(1, 8, n_done, 0)

    def r_done(n, carry):
        for h in range(2):

            @pl.when(jnp.logical_not(r_mine(n, h)))
            def _():
                r_copy(n, h).wait_send()

        return carry

    lax.fori_loop(0, 8, r_done, 0)
    for copy in swaps + halves + [sums]:
        copy.wait_send()
    for p in range(3):
        for k in (1, 2, 3):
            for step in range(2):
                g_copy(step, p, k, False).wait_send()
            for kk in range(4 if p < 2 else 1):
                h_copy(p, kk, k, False).wait_send()
        for m in range(1, 8):
            f_copy(p, m, False).wait_send()
    for p, q in CHUNKS:
        for k in (1, 2, 3):
            c_copy(BASE[p] + q, p, k, False).wait_send()
            b_copy(BASE[p] + q, p, k, False).wait_send()


def on_device(
    hidden,
    q_latent,
    q_rope,
    latent_pages,
    rope_pages,
    block_table,
    cache_len,
    move_req,
    move_to,
    routing,
    gate_weight,
    norm_gain,
    w_uv,
    w_out,
    w_gate,
    w_up,
    w_down,
):
    vmem = pl.BlockSpec(memory_space=pltpu.VMEM)
    smem = pl.BlockSpec(memory_space=pltpu.SMEM)
    hbm = pl.BlockSpec(memory_space=pl.ANY)
    return pl.pallas_call(
        layer,
        out_shape=jax.ShapeDtypeStruct((2, D), BF),
        in_specs=[vmem] * 2 + [smem] * 6 + [hbm] * 9,
        out_specs=vmem,
        scratch_shapes=list(SCRATCH.values()),
        compiler_params=pltpu.CompilerParams(
            collective_id=0, has_side_effects=True, vmem_limit_bytes=56 * 1024 * 1024
        ),
        cost_estimate=pl.CostEstimate(flops=4_000_000_000, bytes_accessed=22_000_000, transcendentals=400_000),
    )(
        hidden,
        norm_gain.reshape(1, D),
        block_table,
        cache_len,
        move_req,
        move_to,
        routing,
        gate_weight,
        q_latent,
        q_rope,
        latent_pages,
        rope_pages,
        w_uv,
        w_out,
        w_gate,
        w_up,
        w_down,
    )


def solution(mesh):
    placed = (
        P(("dp", "ep"), None),
        P(("dp", "ep"), None, None),
        P(("dp", "ep"), None, None),
        P(("dp", "ep"), None, None),
        P(("dp", "ep"), None, None),
        P(("dp", "ep"), None),
        P(("dp", "ep")),
        P(("dp", "ep")),
        P(("dp", "ep")),
        P(("dp", "ep"), None),
        P(("dp", "ep"), None),
        P(),
        P("ep", None, None),
        P("ep", None),
        P("ep", None, "dp"),
        P("ep", None, "dp"),
        P("ep", "dp", None),
    )
    return jax.shard_map(
        on_device, mesh=mesh, in_specs=placed, out_specs=P(("dp", "ep"), None), check_vma=False
    )
```

time: 286 us -> 73.4 us (0.26)
  waiting for transfers between devices: 131 us -> 0 us
  Pallas kernels: 0 us -> 70.4 us
  blocking collectives: 67.1 us -> 0 us
  matrix products: 25.7 us -> 0 us
  local copies, waits for them, and re-layouts: 24.4 us -> 1.38 us
  between operations: 15.6 us -> 1.3 us
  starting transfers between devices: 11.9 us -> 0 us
  other arithmetic: 9.88 us -> 0 us
    unnamed x2 -> x0, waiting for transfers between devices: 79.7 us -> none
    pallas_call x0 -> x1, Pallas kernels: none -> 70.4 us  [on_device(): pl.pallas_call(layer, out_shape=jax.ShapeDtypeStruct((2, D), BF), in_spec...]
    all_to_all x2 -> x0, blocking collectives: 67.1 us -> none  [the longest x1 51.9 us: on_device(): lax.all_to_all(spread, ('dp', 'ep'), split_axis=0, concat_axis=0, tiled=T...]
    all_to_all x2 -> x0, waiting for transfers between devices: 50.8 us -> none  [the longest x1 45.7 us: on_device(): lax.all_to_all(partial_out.reshape(arrived_rows.shape), ('dp', 'ep'), spl...]
    dot_general x10 -> x0, matrix products: 25.7 us -> none  [the longest x1 10 us: on_device(): jnp.dot(inner, w_down[0], preferred_element_type=jnp.float32)]
    reshape x3 -> x0, local copies, waits for them, and re-layouts: 17.6 us -> none  [the longest x1 8.4 us: on_device(): flat_rows = arrived_rows.reshape(-1, model_width)]
    all_to_all x2 -> x0, starting transfers between devices: 11.8 us -> none  [the longest x1 6.29 us: on_device(): lax.all_to_all(row_parcel, 'dp', split_axis=0, concat_axis=0, tiled=True)]
    reduce_sum x5 -> x0, other arithmetic: 6.46 us -> none  [the longest x1 5.66 us: on_device(): jnp.sum(returned.reshape(dp_count, ep_count, capacity, model_width).astyp...]
  transfers between devices with their start and end apart: 3 -> 0, of which waited for: 3 -> 0; matrix products, arithmetic and copies ran while one was open for 0% -> 0% of each run, Pallas kernels for 0% -> 0%
where the time goes in v1:
time: 73.4 us; the launch traced here: 73.1 us
  Pallas kernels  70.4 us (96%)
  local copies, waits for them, and re-layouts  1.38 us (2%)
  between operations  1.3 us (2%)
    pallas_call x1, Pallas kernels, on_device(): pl.pallas_call(layer, out_shape=jax.ShapeDtypeStruct((2, D), BF), in_spec...  70.4 us

profile of v1, /device:TPU:1, one launch (start us, length us, event | category | flops | bytes accessed | tf_op | source)
XLA Modules:
  0.0 73.1 jit_solution(9995842560142864548)
XLA Ops:
  1.3 70.4 %shard_map.163 = bf16[2,7168]{1,0:T(2,128)(2,1)} custom-call(bf16[2,7168]{1,0:T(2,128)(2,1)} %hidden.1, f32[1,7168]{1,0:T(1,128)} %bitcast.1, s32[2,12]{1,0:T(2,128)} %table.1, s32[2]{0:T(128)} %lens.1, s32[1]{0:T(128)S(6)} %copy.19.move_req, s32[1]{0:T(128)S(6)} %copy.20.move_to, s32[2,8]{1,0:T(2,128)} %routing.1, f32[2,8]{1,0:T(2,128)} %gates.1, ...), custom_call_target="tpu_custom_call" | custom-call | flops 4000000000 | bytes 22000000 | tf_op jit(solution)/shard_map/pallas_call | solution.py:650
  71.7 1.4 %copy.21 = bf16[2,7168]{1,0:T(2,128)(2,1)} copy(bf16[2,7168]{1,0:T(2,128)(2,1)} %shard_map.163) | data formatting | bytes 57344

commit v2 on v1

v2 whole, which is shorter than its diff:
```python
import types

import jax
import jax.numpy as jnp
from jax import lax
from jax.experimental import pallas as pl
from jax.experimental.pallas import tpu as pltpu
from jax.sharding import PartitionSpec as P

MESH = pl.DeviceIdType.MESH
BF = jnp.bfloat16
F32 = jnp.float32

D = 7168
HALF = D // 2
BLK = 896
PIECES = (384, 256, 256)
STARTS = (0, 384, 640)
GATHER = (("z", "y", "x"), ("z", "x", "y"), ("x", "y", "z"))
REDUCE = (("x", "y", "z"), ("y", "z", "x"), ("z", "x", "y"))
BASE = (0, 5, 10)
COUNT = (5, 5, 4)
DIRECT = 1
CHUNKS = [(p, q) for q in range(5) for p in range(3) if q < COUNT[p]]

SCRATCH = dict(
    qv=pltpu.VMEM((2, 64, 512), BF),
    qrv=pltpu.VMEM((2, 64, 64), BF),
    pgv=pltpu.VMEM((24, 64, 512), BF),
    rpv=pltpu.VMEM((24, 32, 128), BF),
    uvv=pltpu.VMEM((4, 512, 128), BF),
    wov=pltpu.VMEM((8, 512, BLK), BF),
    wv=pltpu.VMEM((4, HALF, 256), BF),
    wd=pltpu.VMEM((2, 256, HALF), BF),
    scores=pltpu.VMEM((6, 128, 256), F32),
    a_send=pltpu.VMEM((16, 16, 256), BF),
    a_recv=pltpu.VMEM((16, 16, 256), BF),
    ra_send=pltpu.VMEM((16, 16, PIECES[0]), BF),
    rb_send=pltpu.VMEM((16, 16, PIECES[1]), BF),
    rc_send=pltpu.VMEM((16, 16, PIECES[2]), BF),
    ra_recv=pltpu.VMEM((16, 16, PIECES[0]), BF),
    rb_recv=pltpu.VMEM((16, 16, PIECES[1]), BF),
    rc_recv=pltpu.VMEM((16, 16, PIECES[2]), BF),
    m_one=pltpu.VMEM((16, 8, 128), F32),
    m_all=pltpu.VMEM((8, 16, 128), F32),
    xa=pltpu.VMEM((4, 4, 4, 16, PIECES[0]), BF),
    xb=pltpu.VMEM((4, 4, 4, 16, PIECES[1]), BF),
    xc=pltpu.VMEM((4, 4, 4, 16, PIECES[2]), BF),
    xg=pltpu.VMEM((256, BLK), BF),
    pre=pltpu.VMEM((4, 256, 256), F32),
    squares=pltpu.VMEM((256, 128), F32),
    squares_in=pltpu.VMEM((256, 128), F32),
    pre_send=pltpu.VMEM((4, 256, 256), BF),
    pre_recv=pltpu.VMEM((4, 256, 256), BF),
    inner=pltpu.VMEM((2, 256, 256), BF),
    sorted_in=pltpu.VMEM((3, 2, 256, 256), BF),
    perm=pltpu.VMEM((3, 256, 256), BF),
    weight=pltpu.VMEM((3, 256, 128), F32),
    resid=pltpu.VMEM((16, HALF), F32),
    c_send=pltpu.VMEM((14, 4, 64, 256), BF),
    c_recv=pltpu.VMEM((14, 3, 64, 256), BF),
    b_send=pltpu.VMEM((14, 4, 16, 256), BF),
    b_recv=pltpu.VMEM((14, 3, 16, 256), BF),
    f_send=pltpu.VMEM((3, 8, 2, 1280), F32),
    f_recv=pltpu.VMEM((3, 8, 2, 1280), F32),
    d_send=pltpu.VMEM((3, 32, 2, 256 * DIRECT), F32),
    d_recv=pltpu.VMEM((3, 32, 2, 256 * DIRECT), F32),
    load_sem=pltpu.SemaphoreType.DMA((8,)),
    swap_s=pltpu.SemaphoreType.DMA((1,)),
    swap_r=pltpu.SemaphoreType.DMA((2,)),
    half_s=pltpu.SemaphoreType.DMA((2,)),
    half_r=pltpu.SemaphoreType.DMA((3,)),
    spread_s=pltpu.SemaphoreType.DMA((3,)),
    spread_r=pltpu.SemaphoreType.DMA((3,)),
    r_s=pltpu.SemaphoreType.DMA((3,)),
    r_r=pltpu.SemaphoreType.DMA((3,)),
    g_s=pltpu.SemaphoreType.DMA((3,)),
    g_r=pltpu.SemaphoreType.DMA((3, 4)),
    h_s=pltpu.SemaphoreType.DMA((3,)),
    h_r=pltpu.SemaphoreType.DMA((3, 4)),
    c_s=pltpu.SemaphoreType.DMA((1,)),
    c_r=pltpu.SemaphoreType.DMA((14,)),
    b_s=pltpu.SemaphoreType.DMA((1,)),
    b_r=pltpu.SemaphoreType.DMA((14,)),
    f_s=pltpu.SemaphoreType.DMA((3,)),
    f_r=pltpu.SemaphoreType.DMA((3,)),
    d_s=pltpu.SemaphoreType.DMA((3,)),
    d_r=pltpu.SemaphoreType.DMA((3,)),
)


def iota(shape, dim):
    return lax.broadcasted_iota(jnp.int32, shape, dim)


def ones_where(mask):
    return jnp.where(mask, 1.0, 0.0).astype(BF)


def dot(a, b):
    return jnp.dot(a, b, preferred_element_type=F32)


def dot_nt(a, b):
    return lax.dot_general(a, b, (((1,), (1,)), ((), ())), preferred_element_type=F32)


def layer(
    hidden,
    gain,
    table,
    lens,
    move_req,
    move_to,
    routing,
    gates,
    q_latent,
    q_rope,
    pages,
    ropes,
    w_uv,
    w_out,
    w_gate,
    w_up,
    w_down,
    out,
    *scratch,
):
    s = types.SimpleNamespace(**dict(zip(SCRATCH, scratch)))
    i = lax.axis_index("dp")
    j = lax.axis_index("ep")
    x, c = lax.div(i, 2), lax.rem(i, 2)
    z, y = lax.div(j, 4), lax.rem(j, 4)
    other = 1 - c
    at = {"x": x, "y": y, "z": z}

    def place(axis, value, core):
        if axis == "x":
            return (value * 2 + core, j)
        if axis == "y":
            return (x * 2 + core, z * 4 + value)
        return (x * 2 + core, value * 4 + y)

    def turn(axis, k):
        return lax.rem(at[axis] + k, 4)

    def remote(src, dst, send, recv, device):
        return pltpu.make_async_remote_copy(
            src_ref=src, dst_ref=dst, send_sem=send, recv_sem=recv, device_id=device, device_id_type=MESH
        )

    sibling = (x * 2 + other, j)

    def loaded(ref, n):
        pltpu.make_async_copy(ref, ref, s.load_sem.at[n]).wait()

    def arrived(ref, sem):
        remote(ref, ref, sem, sem, sibling).wait_recv()

    def sent(ref, sem):
        remote(ref, ref, sem, sem, sibling).wait_send()

    half = pl.multiple_of(c * HALF, 128)
    others = pl.multiple_of(other * HALF, 128)

    def load(src, dst, n):
        pltpu.make_async_copy(src, dst, s.load_sem.at[n]).start()

    load(q_latent, s.qv, 0)
    load(q_rope, s.qrv, 1)
    load(ropes, s.rpv, 2)
    load(pages, s.pgv, 3)

    barrier = pltpu.get_barrier_semaphore()

    def greet(m, carry):
        t = lax.rem(c * 16 + j + m, 32)
        pl.semaphore_signal(
            barrier, inc=1, device_id=(x * 2 + lax.div(t, 16), lax.rem(t, 16)), device_id_type=MESH
        )
        return carry

    lax.fori_loop(1, 32, greet, 0)
    for k in (1, 2, 3):
        for core in (0, 1):
            pl.semaphore_signal(barrier, inc=1, device_id=place("x", turn("x", k), core), device_id_type=MESH)
        for m in (1, 2, 3):
            for core in (0, 1):
                chip = turn("x", k) * 2 + core
                pl.semaphore_signal(barrier, inc=1, device_id=(chip, turn("z", m) * 4 + y), device_id_type=MESH)
                pl.semaphore_signal(barrier, inc=1, device_id=(chip, z * 4 + turn("y", m)), device_id_type=MESH)

    row = iota((128, 128), 0)
    col = iota((128, 128), 1)
    wanted = lax.rem(lax.div(row, 4), 2) * 64 + lax.div(row, 8) * 4 + lax.rem(row, 4)
    order = ones_where(col == wanted)
    twice = ones_where(iota((64, 128), 0) == lax.rem(iota((64, 128), 1), 64))
    first_row = lax.rem(lax.div(iota((128, 1), 0), 4), 2) == 0
    spread = ones_where(lax.div(iota((256, 128), 0), 2) == iota((256, 128), 1))
    parity = lax.div(iota((256, 128), 1), 64) == lax.rem(iota((256, 128), 0), 2)
    place_of = iota((1, 1536), 1)
    bias = []
    for r in range(2):
        live = jnp.zeros((1, 1536), jnp.int32)
        for q in range(12):
            start = table[r, q] * 64
            count = jnp.clip(lens[r] - q * 64, 0, 64)
            live = jnp.where((place_of >= start) & (place_of < start + count), 1, live)
        bias.append(jnp.where(live > 0, 0.0, -1e30))
    scale = 192.0 ** (-0.5)
    loaded(s.qv, 0)
    loaded(s.qrv, 1)
    query = dot(order, s.qv[...].reshape(128, 512)).astype(BF)
    rotary = dot(dot(order, s.qrv[...].reshape(128, 64)).astype(BF), twice).astype(BF)
    loaded(s.rpv, 2)
    loaded(s.pgv, 3)
    load(w_uv, s.uvv, 4)
    for n in range(8):
        load(w_out.at[:, pl.ds(n * BLK, BLK)], s.wov.at[n], 5)
    load(w_gate.at[0, pl.ds(half, HALF), :], s.wv.at[0], 6)
    load(w_up.at[0, pl.ds(half, HALF), :], s.wv.at[1], 6)
    load(w_down.at[0, :, pl.ds(half, HALF)], s.wd.at[0], 7)
    largest = jnp.full((128, 1), -1e30, F32)
    for n in range(6):
        keys = s.pgv[4 * n : 4 * n + 4].reshape(256, 512)
        turned = dot(spread, s.rpv[4 * n : 4 * n + 4].reshape(128, 128))
        turned = jnp.where(parity, turned, 0.0).astype(BF)
        score = (dot_nt(query, keys) + dot_nt(rotary, turned)) * scale
        cut = slice(256 * n, 256 * n + 256)
        score = score + jnp.where(first_row, bias[0][:, cut], bias[1][:, cut])
        s.scores[n] = score
        largest = jnp.maximum(largest, jnp.max(score, axis=1, keepdims=True))
    total = jnp.zeros((128, 1), F32)
    mixed = jnp.zeros((128, 512), F32)
    for n in range(6):
        prob = jnp.exp(s.scores[n] - largest)
        total = total + jnp.sum(prob, axis=1, keepdims=True)
        mixed = mixed + dot(prob.astype(BF), s.pgv[4 * n : 4 * n + 4].reshape(256, 512))
    mixed = mixed / total
    lower = mixed[:, :256].reshape(16, 8, 256)
    upper = mixed[:, 256:].reshape(16, 8, 256)
    s.a_send[...] = jnp.concatenate([lower, upper], axis=1).astype(BF)
    s.a_recv[j] = s.a_send[j]

    pl.semaphore_wait(barrier, 73)

    def a_copy(k, land):
        t = lax.rem(j + k, 16)
        return remote(s.a_send.at[t], s.a_recv.at[land], s.spread_s.at[0], s.spread_r.at[0], (i, t))

    def a_start(k, carry):
        a_copy(k, j).start()
        return carry

    lax.fori_loop(1, 16, a_start, 0)

    lane = iota((8, 128), 1)
    note = jnp.zeros((8, 128), F32)
    for r in range(2):
        for k in range(8):
            note = jnp.where(lane == routing[r, k] + 16 * r, gates[r, k], note)
    note = jnp.where(lane == 32, move_req[0].astype(F32), note)
    note = jnp.where(lane == 33, move_to[0].astype(F32), note)
    s.m_one[j] = jnp.where(iota((8, 128), 0) == 0, note, 0.0)

    def m_copy(k, land):
        t = lax.rem(j + k, 16)
        return remote(s.m_one.at[land], s.m_one.at[land], s.spread_s.at[1], s.spread_r.at[1], (i, t))

    def m_start(k, carry):
        m_copy(k, j).start()
        return carry

    lax.fori_loop(1, 16, m_start, 0)

    swaps = [
        (w_gate.at[0, pl.ds(others, HALF), :], s.wv.at[2]),
        (w_up.at[0, pl.ds(others, HALF), :], s.wv.at[3]),
        (w_down.at[0, :, pl.ds(others, HALF)], s.wd.at[1]),
    ]
    for n, (src, dst) in enumerate(swaps):
        remote(src, dst, s.swap_s.at[0], s.swap_r.at[n // 2], sibling).start()

    target = iota((256, 256), 0)
    inside = lax.rem(target, 128)
    wanted = (
        lax.div(lax.rem(inside, 32), 2) * 16
        + lax.div(target, 128) * 8
        + lax.rem(inside, 2) * 4
        + lax.div(inside, 32)
    )
    by_head = ones_where(iota((256, 256), 1) == wanted)
    loaded(s.uvv, 4)
    arrived(s.a_recv.at[0:15], s.spread_r.at[0])
    grouped = dot(by_head, s.a_recv[...].reshape(256, 256)).astype(BF)
    values = []
    for h in range(4):
        low = grouped[32 * h : 32 * h + 32]
        high = grouped[128 + 32 * h : 160 + 32 * h]
        values.append((dot(low, s.uvv[h, :256]) + dot(high, s.uvv[h, 256:])).astype(BF))
    values = jnp.concatenate(values, axis=1)
    loaded(s.wov, 5)
    request = iota((32, 1), 0)

    r_send = (s.ra_send, s.rb_send, s.rc_send)
    r_recv = (s.ra_recv, s.rb_recv, s.rc_recv)
    keeps = lax.div(y, 2) == c

    def r_start(p):
        wide = PIECES[p]

        def step(t, carry):
            core, zz = lax.rem(lax.div(t, 4) + y, 2), lax.rem(z + t, 4)
            n = core * 4 + zz
            part = dot(values, s.wov[n, :, STARTS[p] : STARTS[p] + wide])
            own = hidden[:, pl.ds(pl.multiple_of(n * BLK + STARTS[p], 128), wide)].astype(F32)
            part = part + jnp.where(
                request == 2 * j, own[0:1], jnp.where(request == 2 * j + 1, own[1:2], 0.0)
            )
            part = part.astype(BF)
            for h in range(2):
                r_send[p][2 * n + h] = part[16 * h : 16 * h + 16]
            for turned in range(2):
                h = lax.rem(lax.div(y, 2) + turned, 2)
                mine = (core == c) & (zz == z) & (2 * c + h == y)

                @pl.when(jnp.logical_not(mine))
                def _():
                    device = (x * 2 + core, zz * 4 + 2 * c + h)
                    remote(r_send[p].at[2 * n + h], r_recv[p].at[j], s.r_s.at[p], s.r_r.at[p], device).start()

                @pl.when(mine)
                def _():
                    r_recv[p][j] = r_send[p][2 * n + h]

            return carry

        lax.fori_loop(0, 8, step, 0)

    for p in range(3):
        r_start(p)

    arrived(s.m_one.at[0:15], s.spread_r.at[1])
    s.m_all[i] = jnp.sum(s.m_one[...], axis=1)

    def n_copy(k, land):
        t = lax.rem(i + k, 8)
        return remote(s.m_all.at[land], s.m_all.at[land], s.spread_s.at[2], s.spread_r.at[2], (t, j))

    def n_start(k, carry):
        n_copy(k, i).start()
        return carry

    lax.fori_loop(1, 8, n_start, 0)

    pieces = (s.xa, s.xb, s.xc)

    def r_sum(p):
        @pl.when(keeps)
        def _():
            arrived(r_recv[p].at[0:15], s.r_r.at[p])

        @pl.when(jnp.logical_not(keeps))
        def _():
            arrived(r_recv[p], s.r_r.at[p])

        block = r_recv[p][0].astype(F32)
        for t in range(1, 16):
            block = block + r_recv[p][t].astype(F32)
        pieces[p][z, x, y] = block.astype(BF)

    def view(p, where):
        return pieces[p].at[tuple(where.get(a, slice(None)) for a in ("z", "x", "y"))]

    def g_start(p):
        first, second, _ = GATHER[p]
        ref = pieces[p].at[z, x, y]
        for m in (2, 1, 3, 0):
            for k in (2, 1, 3, 0):
                if m or k:
                    to = dict(at)
                    to[first], to[second] = turn(first, m), turn(second, k)
                    device = (to["x"] * 2 + c, to["z"] * 4 + to["y"])
                    remote(ref, ref, s.g_s.at[p], s.g_r.at[p, (4 - m) % 4], device).start()

    def h_start(p, m):
        first, _, axis = GATHER[p]
        arrived(r_recv[p].at[0 : 4 if m else 3], s.g_r.at[p, m])
        ref = view(p, {first: turn(first, m), axis: at[axis]})
        for k in (2, 1, 3):
            recv = s.h_r.at[p, 4 - k if axis == "z" else m]
            remote(ref, ref, s.h_s.at[p], recv, place(axis, turn(axis, k), c)).start()

    r_sum(0)
    g_start(0)
    r_sum(1)
    g_start(1)
    h_start(0, 0)
    r_sum(2)
    g_start(2)
    h_start(0, 1)
    h_start(0, 3)
    h_start(1, 0)
    h_start(0, 2)
    h_start(1, 1)
    h_start(1, 3)
    h_start(2, 0)
    h_start(1, 2)
    h_start(2, 1)
    h_start(2, 3)
    h_start(2, 2)

    arrived(s.m_all.at[0:7], s.spread_r.at[2])
    notes = s.m_all[...].reshape(128, 128)
    notes_high = notes.astype(BF)
    notes_low = (notes - notes_high.astype(F32)).astype(BF)
    picked = dot_nt(ones_where(iota((8, 128), 1) == 32 + iota((8, 128), 0)), notes_high).astype(BF)
    picked = dot(picked, ones_where(lax.div(iota((128, 256), 1), 2) == iota((128, 256), 0)))
    home = iota((1, 256), 1)
    home_key = jnp.where(
        picked[0:1] == lax.rem(home, 2).astype(F32),
        256.0 + picked[1:2] * 16.0 + lax.rem(lax.div(home, 2), 16).astype(F32),
        home.astype(F32),
    )

    def arrange(device, slot):
        size = device.shape[0]
        lanes = iota((size, 128), 1)
        found = ones_where(lanes == device)
        found = dot(found, notes_high) + dot(found, notes_low)
        weigh = jnp.sum(jnp.where(lanes == slot * 16 + j, found, 0.0), axis=1, keepdims=True)
        leaving = jnp.sum(jnp.where(lanes == 32, found, 0.0), axis=1, keepdims=True)
        key = jnp.where(
            leaving == slot.astype(F32), 256.0 + device.astype(F32), (2 * device + slot).astype(F32)
        )
        return ones_where(key == home_key), weigh

    t = iota((256, 1), 0)
    for p in range(3):
        coords = {
            REDUCE[p][0]: lax.div(t, 64),
            REDUCE[p][1]: lax.rem(lax.div(t, 16), 4),
            REDUCE[p][2]: lax.rem(lax.div(t, 4), 4),
        }
        device = (coords["x"] * 2 + lax.rem(lax.div(t, 2), 2)) * 16 + coords["z"] * 4 + coords["y"]
        matrix, weigh = arrange(device, lax.rem(t, 2))
        s.perm[p] = matrix
        s.weight[p] = jnp.broadcast_to(weigh, (256, 128))
    t = iota((16, 1), 0)
    chosen, _ = arrange((x * 2 + lax.rem(lax.div(t, 2), 2)) * 16 + j, lax.rem(t, 2))

    loaded(s.wv.at[0:2], 6)
    arrived(s.wv.at[2:4], s.swap_r.at[0])
    s.pre[...] = jnp.zeros((4, 256, 256), F32)
    s.squares[...] = jnp.zeros((256, 128), F32)

    def project(kk, carry):
        zz = turn("z", kk)
        for p in range(2):
            arrived(pieces[p].at[0, 0:3], s.h_r.at[p, kk])

        @pl.when(kk > 0)
        def _():
            arrived(pieces[2].at[0], s.h_r.at[2, kk])

        squares = s.squares[...]
        for p in range(3):
            rows = pieces[p][zz].reshape(256, PIECES[p]).astype(F32)
            for n in range(PIECES[p] // 128):
                tile = rows[:, 128 * n : 128 * n + 128]
                squares = squares + tile * tile
            width = pl.multiple_of(c * HALF + zz * BLK + STARTS[p], 128)
            s.xg[:, STARTS[p] : STARTS[p] + PIECES[p]] = (
                rows * gain[:, pl.ds(width, PIECES[p])]
            ).astype(BF)
        s.squares[...] = squares
        depth = pl.multiple_of(zz * BLK, 128)
        for m in range(4):
            s.pre[m] = s.pre[m] + dot(s.xg[...], s.wv[m, pl.ds(depth, BLK), :])
        return carry

    lax.fori_loop(0, 4, project, 0)

    remote(s.squares, s.squares_in, s.half_s.at[0], s.half_r.at[0], sibling).start()
    for m in (2, 3, 0, 1):
        t = (m + 2) % 4
        s.pre_send[m] = s.pre[m].astype(BF)
        remote(
            s.pre_send.at[m], s.pre_recv.at[t], s.half_s.at[1], s.half_r.at[1 + t // 2], sibling
        ).start()
    arrived(s.squares_in, s.half_r.at[0])
    square = jnp.sum(s.squares[...] + s.squares_in[...], axis=1, keepdims=True)
    norm = lax.rsqrt(square / D + 1e-06)
    for b in range(2):
        arrived(s.pre_recv.at[2 * b : 2 * b + 2], s.half_r.at[1 + b])
        gate = (s.pre[2 * b] + s.pre_recv[2 * b].astype(F32)) * norm
        up = (s.pre[2 * b + 1] + s.pre_recv[2 * b + 1].astype(F32)) * norm
        s.inner[b] = (gate / (1.0 + jnp.exp(-gate)) * up).astype(BF)
    def c_start(n, p):
        axis = REDUCE[p][0]
        for k in (2, 1, 3):
            src, dst = s.c_send.at[n, turn(axis, k)], s.c_recv.at[n, k - 1]
            remote(src, dst, s.c_s.at[0], s.c_r.at[n], place(axis, turn(axis, k), c)).start()

    def b_start(n, p):
        axis = REDUCE[p][1]
        for k in (2, 1, 3):
            src, dst = s.b_send.at[n, turn(axis, k)], s.b_recv.at[n, k - 1]
            remote(src, dst, s.b_s.at[0], s.b_r.at[n], place(axis, turn(axis, k), c)).start()

    loaded(s.wd.at[0], 7)
    arrived(s.wd.at[1], s.swap_r.at[1])
    for p, q in CHUNKS:
        n = BASE[p] + q
        if q == 0:
            weigh = s.weight[p][:, 0:1]
            for b in range(2):
                s.sorted_in[p, b] = (dot(s.perm[p], s.inner[b]) * weigh).astype(BF)
        cols = slice(256 * n, 256 * n + 256)
        part = dot(s.sorted_in[p, 0], s.wd[0, :, cols]) + dot(s.sorted_in[p, 1], s.wd[1, :, cols])
        s.c_send[n] = part.astype(BF).reshape(4, 64, 256)
        c_start(n, p)

    for p in range(3):
        for zz in range(4):
            begin = zz * BLK + STARTS[p]
            s.resid[:, begin : begin + PIECES[p]] = dot(chosen, pieces[p][zz].reshape(256, PIECES[p]))

    quarter = lax.div(iota((64, 1), 0), 4)

    def d_start(p):
        axis, first, second = REDUCE[p]
        mine = (at[first] * 4 + at[second]) * 2 + c

        def step(m, carry):
            t = lax.rem(mine + m, 32)
            to = {axis: at[axis], first: lax.div(t, 8), second: lax.rem(lax.div(t, 2), 4)}
            device = (to["x"] * 2 + lax.rem(t, 2), to["z"] * 4 + to["y"])
            remote(s.d_send.at[p, t], s.d_recv.at[p, mine], s.d_s.at[p], s.d_r.at[p], device).start()
            return carry

        lax.fori_loop(1, 32, step, 0)
        s.d_recv[p, mine] = s.d_send[p, mine]

    for p, q in CHUNKS:
        n = BASE[p] + q
        axis = REDUCE[p][0]
        arrived(s.c_recv.at[n], s.c_r.at[n])
        part = s.c_send[n, at[axis]].astype(F32)
        for k in range(3):
            part = part + s.c_recv[n, k].astype(F32)
        if q < COUNT[p] - DIRECT:
            s.b_send[n] = part.astype(BF).reshape(4, 16, 256)
            b_start(n, p)
            continue
        stays = jnp.concatenate([s.resid[:, 256 * n : 256 * n + 256]] * 4, axis=0)
        part = part + jnp.where(quarter == at[REDUCE[p][1]] * 4 + at[REDUCE[p][2]], stays, 0.0)
        begin = 256 * (q + DIRECT - COUNT[p])
        for t in range(32):
            s.d_send[p, t, :, begin : begin + 256] = part[2 * t : 2 * t + 2]
        if q == COUNT[p] - 1:
            d_start(p)

    def f_start(p):
        mine = at[REDUCE[p][2]] * 2 + c
        wide = pl.ds(0, (COUNT[p] - DIRECT) * 256)
        for m in range(1, 8):
            t = lax.rem(mine + m, 8)
            src, dst = s.f_send.at[p, t, :, wide], s.f_recv.at[p, mine, :, wide]
            device = place(REDUCE[p][2], lax.div(t, 2), lax.rem(t, 2))
            remote(src, dst, s.f_s.at[p], s.f_r.at[p], device).start()
        s.f_recv[p, mine] = s.f_send[p, mine]

    last = lax.div(iota((16, 1), 0), 4)
    for p, q in CHUNKS:
        if q >= COUNT[p] - DIRECT:
            continue
        n = BASE[p] + q
        arrived(s.b_recv.at[n], s.b_r.at[n])
        part = s.b_send[n, at[REDUCE[p][1]]].astype(F32)
        for k in range(3):
            part = part + s.b_recv[n, k].astype(F32)
        part = part + jnp.where(last == at[REDUCE[p][2]], s.resid[:, 256 * n : 256 * n + 256], 0.0)
        for t in range(8):
            s.f_send[p, t, :, 256 * q : 256 * q + 256] = part[2 * t : 2 * t + 2]
        if q == COUNT[p] - DIRECT - 1:
            f_start(p)
    for p in (2, 0, 1):
        wide = (COUNT[p] - DIRECT) * 256
        arrived(s.f_recv.at[p, 0:7, :, pl.ds(0, wide)], s.f_r.at[p])
        for core in range(2):
            part = s.f_recv[p, core]
            for t in range(1, 4):
                part = part + s.f_recv[p, 2 * t + core]
            begin = core * HALF + BASE[p] * 256
            out[:, begin : begin + wide] = part[:, :wide].astype(BF)
    for p in (2, 0, 1):
        arrived(s.d_recv.at[p, 0:31], s.d_r.at[p])
        for core in range(2):
            part = s.d_recv[p, core]
            for t in range(1, 16):
                part = part + s.d_recv[p, 2 * t + core]
            begin = core * HALF + (BASE[p] + COUNT[p] - DIRECT) * 256
            out[:, begin : begin + 256 * DIRECT] = part.astype(BF)

    sent(s.a_send.at[0:15], s.spread_s.at[0])
    sent(s.m_one.at[0:15], s.spread_s.at[1])
    sent(s.m_all.at[0:7], s.spread_s.at[2])

    for p in range(3):

        @pl.when(keeps)
        def _():
            sent(r_send[p].at[0:15], s.r_s.at[p])

        @pl.when(jnp.logical_not(keeps))
        def _():
            sent(r_send[p], s.r_s.at[p])

    sent(s.wv.at[0:3], s.swap_s.at[0])
    sent(s.squares, s.half_s.at[0])
    sent(s.pre_send, s.half_s.at[1])
    for p in range(3):
        sent(r_recv[p].at[0:15], s.g_s.at[p])
        sent(pieces[p].at[0:3], s.h_s.at[p])
        sent(s.f_send.at[p, 0:7, :, pl.ds(0, (COUNT[p] - DIRECT) * 256)], s.f_s.at[p])
        sent(s.d_send.at[p, 0:31], s.d_s.at[p])
    sent(s.c_send.at[:, 0:3], s.c_s.at[0])
    sent(s.b_send.at[0 : 14 - 3 * DIRECT, 0:3], s.b_s.at[0])


def on_device(
    hidden,
    q_latent,
    q_rope,
    latent_pages,
    rope_pages,
    block_table,
    cache_len,
    move_req,
    move_to,
    routing,
    gate_weight,
    norm_gain,
    w_uv,
    w_out,
    w_gate,
    w_up,
    w_down,
):
    vmem = pl.BlockSpec(memory_space=pltpu.VMEM)
    smem = pl.BlockSpec(memory_space=pltpu.SMEM)
    hbm = pl.BlockSpec(memory_space=pl.ANY)
    return pl.pallas_call(
        layer,
        out_shape=jax.ShapeDtypeStruct((2, D), BF),
        in_specs=[vmem] * 2 + [smem] * 6 + [hbm] * 9,
        out_specs=vmem,
        scratch_shapes=list(SCRATCH.values()),
        compiler_params=pltpu.CompilerParams(
            collective_id=0, has_side_effects=True, vmem_limit_bytes=56 * 1024 * 1024
        ),
        cost_estimate=pl.CostEstimate(flops=4_000_000_000, bytes_accessed=22_000_000, transcendentals=400_000),
    )(
        hidden,
        norm_gain.reshape(1, D),
        block_table,
        cache_len,
        move_req,
        move_to,
        routing,
        gate_weight,
        q_latent,
        q_rope,
        latent_pages,
        rope_pages,
        w_uv,
        w_out,
        w_gate,
        w_up,
        w_down,
    )


def solution(mesh):
    placed = (
        P(("dp", "ep"), None),
        P(("dp", "ep"), None, None),
        P(("dp", "ep"), None, None),
        P(("dp", "ep"), None, None),
        P(("dp", "ep"), None, None),
        P(("dp", "ep"), None),
        P(("dp", "ep")),
        P(("dp", "ep")),
        P(("dp", "ep")),
        P(("dp", "ep"), None),
        P(("dp", "ep"), None),
        P(),
        P("ep", None, None),
        P("ep", None),
        P("ep", None, "dp"),
        P("ep", None, "dp"),
        P("ep", "dp", None),
    )
    return jax.shard_map(
        on_device, mesh=mesh, in_specs=placed, out_specs=P(("dp", "ep"), None), check_vma=False
    )
```

time: 73.4 us -> 63.6 us (0.87)
  Pallas kernels: 70.4 us -> 60.7 us
    pallas_call x1, Pallas kernels: 70.4 us -> 60.7 us  [on_device(): pl.pallas_call(layer, out_shape=jax.ShapeDtypeStruct((2, D), BF), in_spec...]
where the time goes in v2:
time: 63.6 us; the launch traced here: 63.4 us
  Pallas kernels  60.7 us (95%)
  local copies, waits for them, and re-layouts  1.38 us (2%)
  between operations  1.3 us (2%)
    pallas_call x1, Pallas kernels, on_device(): pl.pallas_call(layer, out_shape=jax.ShapeDtypeStruct((2, D), BF), in_spec...  60.7 us
    unnamed x1, local copies, waits for them, and re-layouts  1.38 us

profile of v2, /device:TPU:1, one launch (start us, length us, event | category | flops | bytes accessed | tf_op | source)
XLA Modules:
  0.0 63.4 jit_solution(18346139956792795472)
XLA Ops:
  1.3 60.7 %shard_map.163 = bf16[2,7168]{1,0:T(2,128)(2,1)} custom-call(bf16[2,7168]{1,0:T(2,128)(2,1)} %hidden.1, f32[1,7168]{1,0:T(1,128)} %bitcast.1, s32[2,12]{1,0:T(2,128)} %table.1, s32[2]{0:T(128)} %lens.1, s32[1]{0:T(128)S(6)} %copy.19.move_req, s32[1]{0:T(128)S(6)} %copy.20.move_to, s32[2,8]{1,0:T(2,128)} %routing.1, f32[2,8]{1,0:T(2,128)} %gates.1, ...), custom_call_target="tpu_custom_call" | custom-call | flops 4000000000 | bytes 22000000 | tf_op jit(solution)/shard_map/pallas_call | solution.py:654
  62.0 1.4 %copy.21 = bf16[2,7168]{1,0:T(2,128)(2,1)} copy(bf16[2,7168]{1,0:T(2,128)(2,1)} %shard_map.163) | data formatting | bytes 57344

commit v3 on v2

--- a/solution.py
+++ b/solution.py
@@ -14,9 +14,9 @@
 D = 7168
 HALF = D // 2
 BLK = 896
-PIECES = (384, 256, 256)
-STARTS = (0, 384, 640)
-GATHER = (("z", "y", "x"), ("z", "x", "y"), ("x", "y", "z"))
+PIECES = (256, 128, 256, 256)
+STARTS = (0, 256, 384, 640)
+GATHER = (("z", "y", "x"), ("z", "x", "y"), ("z", "x", "y"), ("x", "y", "z"))
 REDUCE = (("x", "y", "z"), ("y", "z", "x"), ("z", "x", "y"))
 BASE = (0, 5, 10)
 COUNT = (5, 5, 4)
@@ -38,14 +38,17 @@
     ra_send=pltpu.VMEM((16, 16, PIECES[0]), BF),
     rb_send=pltpu.VMEM((16, 16, PIECES[1]), BF),
     rc_send=pltpu.VMEM((16, 16, PIECES[2]), BF),
+    rd_send=pltpu.VMEM((16, 16, PIECES[3]), BF),
     ra_recv=pltpu.VMEM((16, 16, PIECES[0]), BF),
     rb_recv=pltpu.VMEM((16, 16, PIECES[1]), BF),
     rc_recv=pltpu.VMEM((16, 16, PIECES[2]), BF),
+    rd_recv=pltpu.VMEM((16, 16, PIECES[3]), BF),
     m_one=pltpu.VMEM((16, 8, 128), F32),
     m_all=pltpu.VMEM((8, 16, 128), F32),
     xa=pltpu.VMEM((4, 4, 4, 16, PIECES[0]), BF),
     xb=pltpu.VMEM((4, 4, 4, 16, PIECES[1]), BF),
     xc=pltpu.VMEM((4, 4, 4, 16, PIECES[2]), BF),
+    xd=pltpu.VMEM((4, 4, 4, 16, PIECES[3]), BF),
     xg=pltpu.VMEM((256, BLK), BF),
     pre=pltpu.VMEM((4, 256, 256), F32),
     squares=pltpu.VMEM((256, 128), F32),
@@ -72,12 +75,12 @@
     half_r=pltpu.SemaphoreType.DMA((3,)),
     spread_s=pltpu.SemaphoreType.DMA((3,)),
     spread_r=pltpu.SemaphoreType.DMA((3,)),
-    r_s=pltpu.SemaphoreType.DMA((3,)),
-    r_r=pltpu.SemaphoreType.DMA((3,)),
-    g_s=pltpu.SemaphoreType.DMA((3,)),
-    g_r=pltpu.SemaphoreType.DMA((3, 4)),
-    h_s=pltpu.SemaphoreType.DMA((3,)),
-    h_r=pltpu.SemaphoreType.DMA((3, 4)),
+    r_s=pltpu.SemaphoreType.DMA((4,)),
+    r_r=pltpu.SemaphoreType.DMA((4,)),
+    g_s=pltpu.SemaphoreType.DMA((4,)),
+    g_r=pltpu.SemaphoreType.DMA((4, 4)),
+    h_s=pltpu.SemaphoreType.DMA((4,)),
+    h_r=pltpu.SemaphoreType.DMA((4, 4)),
     c_s=pltpu.SemaphoreType.DMA((1,)),
     c_r=pltpu.SemaphoreType.DMA((14,)),
     b_s=pltpu.SemaphoreType.DMA((1,)),
@@ -302,8 +305,8 @@
     loaded(s.wov, 5)
     request = iota((32, 1), 0)
 
-    r_send = (s.ra_send, s.rb_send, s.rc_send)
-    r_recv = (s.ra_recv, s.rb_recv, s.rc_recv)
+    r_send = (s.ra_send, s.rb_send, s.rc_send, s.rd_send)
+    r_recv = (s.ra_recv, s.rb_recv, s.rc_recv, s.rd_recv)
     keeps = lax.div(y, 2) == c
 
     def r_start(p):
@@ -337,7 +340,7 @@
 
         lax.fori_loop(0, 8, step, 0)
 
-    for p in range(3):
+    for p in range(4):
         r_start(p)
 
     arrived(s.m_one.at[0:15], s.spread_r.at[1])
@@ -353,7 +356,7 @@
 
     lax.fori_loop(1, 8, n_start, 0)
 
-    pieces = (s.xa, s.xb, s.xc)
+    pieces = (s.xa, s.xb, s.xc, s.xd)
 
     def r_sum(p):
         @pl.when(keeps)
@@ -395,20 +398,19 @@
     g_start(0)
     r_sum(1)
     g_start(1)
-    h_start(0, 0)
     r_sum(2)
     g_start(2)
-    h_start(0, 1)
-    h_start(0, 3)
+    h_start(0, 0)
     h_start(1, 0)
-    h_start(0, 2)
-    h_start(1, 1)
-    h_start(1, 3)
-    h_start(2, 0)
-    h_start(1, 2)
-    h_start(2, 1)
-    h_start(2, 3)
-    h_start(2, 2)
+    r_sum(3)
+    g_start(3)
+    for m in (1, 3, 2):
+        h_start(0, m)
+        h_start(1, m)
+    for m in (0, 1, 3, 2):
+        h_start(2, m)
+    for m in (0, 1, 3, 2):
+        h_start(3, m)
 
     arrived(s.m_all.at[0:7], s.spread_r.at[2])
     notes = s.m_all[...].reshape(128, 128)
@@ -454,17 +456,18 @@
     s.pre[...] = jnp.zeros((4, 256, 256), F32)
     s.squares[...] = jnp.zeros((256, 128), F32)
 
-    def project(kk, carry):
+    def project(step, carry):
+        kk = step + lax.div(step, 2) - 2 * lax.div(step, 3)
         zz = turn("z", kk)
-        for p in range(2):
+        for p in range(3):
             arrived(pieces[p].at[0, 0:3], s.h_r.at[p, kk])
 
         @pl.when(kk > 0)
         def _():
-            arrived(pieces[2].at[0], s.h_r.at[2, kk])
+            arrived(pieces[3].at[0], s.h_r.at[3, kk])
 
         squares = s.squares[...]
-        for p in range(3):
+        for p in range(4):
             rows = pieces[p][zz].reshape(256, PIECES[p]).astype(F32)
             for n in range(PIECES[p] // 128):
                 tile = rows[:, 128 * n : 128 * n + 128]
@@ -521,7 +524,7 @@
         s.c_send[n] = part.astype(BF).reshape(4, 64, 256)
         c_start(n, p)
 
-    for p in range(3):
+    for p in range(4):
         for zz in range(4):
             begin = zz * BLK + STARTS[p]
             s.resid[:, begin : begin + PIECES[p]] = dot(chosen, pieces[p][zz].reshape(256, PIECES[p]))
@@ -607,7 +610,7 @@
     sent(s.m_one.at[0:15], s.spread_s.at[1])
     sent(s.m_all.at[0:7], s.spread_s.at[2])
 
-    for p in range(3):
+    for p in range(4):
 
         @pl.when(keeps)
         def _():
@@ -621,10 +624,11 @@
     sent(s.squares, s.half_s.at[0])
     sent(s.pre_send, s.half_s.at[1])
     for p in range(3):
+        sent(s.f_send.at[p, 0:7, :, pl.ds(0, (COUNT[p] - DIRECT) * 256)], s.f_s.at[p])
+        sent(s.d_send.at[p, 0:31], s.d_s.at[p])
+    for p in range(4):
         sent(r_recv[p].at[0:15], s.g_s.at[p])
         sent(pieces[p].at[0:3], s.h_s.at[p])
-        sent(s.f_send.at[p, 0:7, :, pl.ds(0, (COUNT[p] - DIRECT) * 256)], s.f_s.at[p])
-        sent(s.d_send.at[p, 0:31], s.d_s.at[p])
     sent(s.c_send.at[:, 0:3], s.c_s.at[0])
     sent(s.b_send.at[0 : 14 - 3 * DIRECT, 0:3], s.b_s.at[0])
 

time: 63.6 us -> 62.7 us (0.986)
  Pallas kernels: 60.7 us -> 59.8 us
    pallas_call x1, Pallas kernels: 60.7 us -> 59.8 us  [on_device(): pl.pallas_call(layer, out_shape=jax.ShapeDtypeStruct((2, D), BF), in_spec...]
where the time goes in v3:
time: 62.7 us; the launch traced here: 62.5 us
  Pallas kernels  59.8 us (95%)
  local copies, waits for them, and re-layouts  1.38 us (2%)
  between operations  1.3 us (2%)
    pallas_call x1, Pallas kernels, on_device(): pl.pallas_call(layer, out_shape=jax.ShapeDtypeStruct((2, D), BF), in_spec...  59.8 us
    unnamed x1, local copies, waits for them, and re-layouts  1.38 us

profile of v3, /device:TPU:1, one launch (start us, length us, event | category | flops | bytes accessed | tf_op | source)
XLA Modules:
  0.0 62.5 jit_solution(1457217036463432407)
XLA Ops:
  1.3 59.8 %shard_map.163 = bf16[2,7168]{1,0:T(2,128)(2,1)} custom-call(bf16[2,7168]{1,0:T(2,128)(2,1)} %hidden.1, f32[1,7168]{1,0:T(1,128)} %bitcast.1, s32[2,12]{1,0:T(2,128)} %table.1, s32[2]{0:T(128)} %lens.1, s32[1]{0:T(128)S(6)} %copy.19.move_req, s32[1]{0:T(128)S(6)} %copy.20.move_to, s32[2,8]{1,0:T(2,128)} %routing.1, f32[2,8]{1,0:T(2,128)} %gates.1, ...), custom_call_target="tpu_custom_call" | custom-call | flops 4000000000 | bytes 22000000 | tf_op jit(solution)/shard_map/pallas_call | solution.py:658
  61.1 1.4 %copy.21 = bf16[2,7168]{1,0:T(2,128)(2,1)} copy(bf16[2,7168]{1,0:T(2,128)(2,1)} %shard_map.163) | data formatting | bytes 57344

commit v4 on v3

--- a/solution.py
+++ b/solution.py
@@ -394,23 +394,13 @@
             recv = s.h_r.at[p, 4 - k if axis == "z" else m]
             remote(ref, ref, s.h_s.at[p], recv, place(axis, turn(axis, k), c)).start()
 
-    r_sum(0)
-    g_start(0)
-    r_sum(1)
-    g_start(1)
-    r_sum(2)
-    g_start(2)
-    h_start(0, 0)
-    h_start(1, 0)
-    r_sum(3)
-    g_start(3)
-    for m in (1, 3, 2):
-        h_start(0, m)
-        h_start(1, m)
-    for m in (0, 1, 3, 2):
-        h_start(2, m)
-    for m in (0, 1, 3, 2):
-        h_start(3, m)
+    for p in range(4):
+        r_sum(p)
+        g_start(p)
+    for p, m in ((0, 0), (1, 0), (0, 1), (1, 1), (0, 3), (1, 3), (2, 0), (0, 2), (1, 2), (2, 1), (2, 3), (3, 0)):
+        h_start(p, m)
+    for p, m in ((2, 2), (3, 1), (3, 3), (3, 2)):
+        h_start(p, m)
 
     arrived(s.m_all.at[0:7], s.spread_r.at[2])
     notes = s.m_all[...].reshape(128, 128)

time: 62.7 us -> 62.5 us (level)
  no operation moved by 1% of the time
where the time goes in v4:
time: 62.5 us; the launch traced here: 62.3 us
  Pallas kernels  59.6 us (95%)
  local copies, waits for them, and re-layouts  1.38 us (2%)
  between operations  1.3 us (2%)
    pallas_call x1, Pallas kernels, on_device(): pl.pallas_call(layer, out_shape=jax.ShapeDtypeStruct((2, D), BF), in_spec...  59.6 us
    unnamed x1, local copies, waits for them, and re-layouts  1.38 us

profile of v4, /device:TPU:1, one launch (start us, length us, event | category | flops | bytes accessed | tf_op | source)
XLA Modules:
  0.0 62.3 jit_solution(17638177309644182608)
XLA Ops:
  1.3 59.6 %shard_map.163 = bf16[2,7168]{1,0:T(2,128)(2,1)} custom-call(bf16[2,7168]{1,0:T(2,128)(2,1)} %hidden.1, f32[1,7168]{1,0:T(1,128)} %bitcast.1, s32[2,12]{1,0:T(2,128)} %table.1, s32[2]{0:T(128)} %lens.1, s32[1]{0:T(128)S(6)} %copy.19.move_req, s32[1]{0:T(128)S(6)} %copy.20.move_to, s32[2,8]{1,0:T(2,128)} %routing.1, f32[2,8]{1,0:T(2,128)} %gates.1, ...), custom_call_target="tpu_custom_call" | custom-call | flops 4000000000 | bytes 22000000 | tf_op jit(solution)/shard_map/pallas_call | solution.py:648
  60.9 1.4 %copy.21 = bf16[2,7168]{1,0:T(2,128)(2,1)} copy(bf16[2,7168]{1,0:T(2,128)(2,1)} %shard_map.163) | data formatting | bytes 57344

commit v5 on v4

--- a/solution.py
+++ b/solution.py
@@ -176,14 +176,10 @@
 
     barrier = pltpu.get_barrier_semaphore()
 
-    def greet(m, carry):
-        t = lax.rem(c * 16 + j + m, 32)
-        pl.semaphore_signal(
-            barrier, inc=1, device_id=(x * 2 + lax.div(t, 16), lax.rem(t, 16)), device_id_type=MESH
-        )
-        return carry
-
-    lax.fori_loop(1, 32, greet, 0)
+    for m in range(1, 16):
+        pl.semaphore_signal(barrier, inc=1, device_id=(i, lax.rem(j + m, 16)), device_id_type=MESH)
+    for m in range(16):
+        pl.semaphore_signal(barrier, inc=1, device_id=(x * 2 + other, m), device_id_type=MESH)
     for k in (1, 2, 3):
         for core in (0, 1):
             pl.semaphore_signal(barrier, inc=1, device_id=place("x", turn("x", k), core), device_id_type=MESH)
@@ -251,11 +247,8 @@
         t = lax.rem(j + k, 16)
         return remote(s.a_send.at[t], s.a_recv.at[land], s.spread_s.at[0], s.spread_r.at[0], (i, t))
 
-    def a_start(k, carry):
+    for k in range(1, 16):
         a_copy(k, j).start()
-        return carry
-
-    lax.fori_loop(1, 16, a_start, 0)
 
     lane = iota((8, 128), 1)
     note = jnp.zeros((8, 128), F32)

time: 62.5 us -> 62.1 us (level)
  no operation moved by 1% of the time
where the time goes in v5:
time: 62.1 us; the launch traced here: 61.8 us
  Pallas kernels  59.1 us (95%)
  local copies, waits for them, and re-layouts  1.38 us (2%)
  between operations  1.3 us (2%)
    pallas_call x1, Pallas kernels, on_device(): pl.pallas_call(layer, out_shape=jax.ShapeDtypeStruct((2, D), BF), in_spec...  59.1 us
    unnamed x1, local copies, waits for them, and re-layouts  1.38 us

profile of v5, /device:TPU:1, one launch (start us, length us, event | category | flops | bytes accessed | tf_op | source)
XLA Modules:
  0.0 61.8 jit_solution(9665835776412994401)
XLA Ops:
  1.3 59.1 %shard_map.163 = bf16[2,7168]{1,0:T(2,128)(2,1)} custom-call(bf16[2,7168]{1,0:T(2,128)(2,1)} %hidden.1, f32[1,7168]{1,0:T(1,128)} %bitcast.1, s32[2,12]{1,0:T(2,128)} %table.1, s32[2]{0:T(128)} %lens.1, s32[1]{0:T(128)S(6)} %copy.19.move_req, s32[1]{0:T(128)S(6)} %copy.20.move_to, s32[2,8]{1,0:T(2,128)} %routing.1, f32[2,8]{1,0:T(2,128)} %gates.1, ...), custom_call_target="tpu_custom_call" | custom-call | flops 4000000000 | bytes 22000000 | tf_op jit(solution)/shard_map/pallas_call | solution.py:641
  60.4 1.4 %copy.21 = bf16[2,7168]{1,0:T(2,128)(2,1)} copy(bf16[2,7168]{1,0:T(2,128)(2,1)} %shard_map.163) | data formatting | bytes 57344
